TPU v7x, 32 devices: a whole 2x2x4 slice. The times are simulated.
32 devices in a mesh: section: 4 (over y, x), fork: 8 (over z, core).
Axes of the slice: x: 2, y: 2, z: 4, core: 2. Of those that a mesh axis runs over, the one named last changes fastest.
Arguments:
- arriving: bfloat16 [4, 8, 128, 4096], P('section', 'fork'), may hold values from -6 to 6
- saved_input: bfloat16 [4, 8, 128, 4096], P('section', 'fork'), may hold values from -6 to 6
- returning: bfloat16 [4, 8, 128, 4096], P('section', 'fork'), may hold values from -6 to 6
- prompt_cache: bfloat16 [4, 2, 512, 512], P('section', None, 'fork'), may hold values from -20 to 20
- fresh_cache: bfloat16 [4, 8, 2, 128, 512], P('section', 'fork'), may hold values from -6 to 6
- back_cache: bfloat16 [4, 8, 2, 128, 512], P('section', 'fork'), may hold values from -6 to 6
- query_gain: float32 [4, 4096], P('section'), may hold values from 0.25 to 1.75
- block_tables: int32 [8, 16], P('fork'), may hold values from 0 to 31, as said below
- fresh_lengths: int32 [8], P('fork'), may hold values from 32 to 128
- back_lengths: int32 [8], P('fork'), may hold values from 32 to 128
Outputs:
- section_output: bfloat16 [4, 8, 128, 4096], P('section', 'fork')
- input_grad: bfloat16 [4, 8, 128, 4096], P('section', 'fork')
- prompt_grad: float32 [4, 2, 512, 512], P('section', None, 'fork')
- completion_grad: float32 [4, 8, 2, 128, 512], P('section', 'fork')
- gain_grad: float32 [4, 4096], P('section')
Inputs may be any that keep to these rules, and one draw needn't show every extreme that they name: `block_tables`: completions 0 to 3 read one prompt and the others a second one: each row lists that prompt's 16 pool blocks in order, the same row for all completions of a prompt; the two prompts' blocks are distinct and together fill the pool.
All inputs are finite; a program needn't handle non-finite values.
Results may differ from a plain program's by a relative error of at most 0.0023.
The roundings to bfloat16 on the way count: a program that leaves them out, or rounds other values in their place, can miss the bound.
Values may be sent and summed in bfloat16 or wider, within the bound.
A program may use at most 128 MiB of HBM per device.

v0:
```python
import jax
import jax.numpy as jnp
from jax import lax
from jax.sharding import PartitionSpec as P

KV = 4
HD = 128
BLOCK = 16


epsilon = 1e-06
masked_score = -1e30


def shifted_2(value, axis, steps):
    count = lax.axis_size(axis)
    pairs = [(source, (source + steps) % count) for source in range(count)]
    return lax.ppermute(value, axis, pairs)


def normed(x_rows, gain_row):
    floated = x_rows.astype(jnp.float32)
    inverse = lax.rsqrt(jnp.mean(floated * floated, axis=-1, keepdims=True) + epsilon)
    return ((floated * inverse * gain_row).astype(jnp.bfloat16), floated, inverse)


def visible_keys(row_count, prompt_count, length):
    places = jnp.arange(row_count, dtype=jnp.int32)
    recent = (places[None, :] <= places[:, None]) & (places[None, :] < length)
    return jnp.concatenate([jnp.ones((row_count, prompt_count), dtype=bool), recent], axis=1)


def by_group(array):
    return array.reshape(array.shape[0], KV, -1).transpose(1, 0, 2)


def softmax_rows(q_group, k_group, key_mask):
    row_count = q_group.shape[0]
    head_rows = q_group.reshape(row_count, -1, HD)
    scores = jnp.einsum(
        "ihd,td->hit", head_rows, k_group, preferred_element_type=jnp.float32
    ) * HD ** (-0.5)
    scores = jnp.where(key_mask[None], scores, masked_score)
    shifted = jnp.exp(scores - jnp.max(scores, axis=-1, keepdims=True))
    return (shifted / jnp.sum(shifted, axis=-1, keepdims=True), head_rows)


def prompt_rows(block_pool, block_table):
    blocks = block_pool.reshape(2, -1, BLOCK, block_pool.shape[-1])
    picked = jnp.take(blocks, block_table, axis=1).reshape(2, -1, block_pool.shape[-1])
    return (picked[0], picked[1])


def forward_layer(x_rows, gain_row, prompt_keys, prompt_values, own_cache, length):
    queries, floated, inverse = normed(x_rows, gain_row)
    row_count = x_rows.shape[0]
    all_keys = jnp.concatenate([prompt_keys, own_cache[0]], axis=0)
    all_values = jnp.concatenate([prompt_values, own_cache[1]], axis=0)
    key_mask = visible_keys(row_count, prompt_keys.shape[0], length)

    def forward_per_group(pieces):
        q_group, k_group, v_group = pieces
        chances, head_rows = softmax_rows(q_group, k_group, key_mask)
        rounded = chances.astype(jnp.bfloat16)
        return jnp.einsum(
            "hit,td->ihd", rounded, v_group, preferred_element_type=jnp.float32
        ).reshape(row_count, -1)

    results = lax.map(
        forward_per_group, (by_group(queries), by_group(all_keys), by_group(all_values))
    )
    attended = results.transpose(1, 0, 2).reshape(row_count, -1)
    valid_rows = (jnp.arange(row_count, dtype=jnp.int32) < length).astype(jnp.float32)[:, None]
    return (floated + valid_rows * attended).astype(jnp.bfloat16)


def backward_layer(x_rows, gain_row, prompt_keys, prompt_values, own_cache, length, cotangent):
    queries, floated, inverse = normed(x_rows, gain_row)
    row_count = x_rows.shape[0]
    prompt_count = prompt_keys.shape[0]
    all_keys = jnp.concatenate([prompt_keys, own_cache[0]], axis=0)
    all_values = jnp.concatenate([prompt_values, own_cache[1]], axis=0)
    key_mask = visible_keys(row_count, prompt_count, length)
    valid_rows = (jnp.arange(row_count, dtype=jnp.int32) < length).astype(jnp.float32)[:, None]
    grad_float = cotangent.astype(jnp.float32)
    out_grad = (valid_rows * grad_float).astype(jnp.bfloat16)

    def backward_per_group(pieces):
        q_group, k_group, v_group, d_group = pieces
        chances, head_rows = softmax_rows(q_group, k_group, key_mask)
        rounded = chances.astype(jnp.bfloat16)
        d_out = d_group.reshape(row_count, -1, HD)
        d_value = jnp.einsum("hit,ihd->td", rounded, d_out, preferred_element_type=jnp.float32)
        d_weight = jnp.einsum("ihd,td->hit", d_out, v_group, preferred_element_type=jnp.float32)
        row_delta = jnp.sum(chances * d_weight, axis=-1, keepdims=True)
        d_score = (chances * (d_weight - row_delta) * HD ** (-0.5)).astype(jnp.bfloat16)
        d_query = jnp.einsum(
            "hit,td->ihd", d_score, k_group, preferred_element_type=jnp.float32
        ).reshape(row_count, -1)
        d_key = jnp.einsum("hit,ihd->td", d_score, head_rows, preferred_element_type=jnp.float32)
        return (d_query, d_key, d_value)

    d_query, d_key, d_value = lax.map(
        backward_per_group,
        (by_group(queries), by_group(all_keys), by_group(all_values), by_group(out_grad)),
    )
    d_query = d_query.transpose(1, 0, 2).reshape(row_count, -1)
    d_key = d_key.transpose(1, 0, 2).reshape(all_keys.shape[0], -1)
    d_value = d_value.transpose(1, 0, 2).reshape(all_keys.shape[0], -1)
    d_normed = d_query * gain_row
    d_input = inverse * d_normed - floated * inverse**3 * jnp.mean(
        d_normed * floated, axis=-1, keepdims=True
    )
    gain_part = jnp.sum(d_query * floated * inverse, axis=0)
    own_grad = jnp.stack([d_key[prompt_count:], d_value[prompt_count:]])
    shared_grad = jnp.stack([d_key[:prompt_count], d_value[:prompt_count]])
    return ((grad_float + d_input).astype(jnp.bfloat16), own_grad, shared_grad, gain_part)


def shards(
    arriving,
    saved_input,
    returning,
    prompt_cache,
    fresh_cache,
    back_cache,
    query_gain,
    block_tables,
    fresh_lengths,
    back_lengths,
):
    incoming = shifted_2(arriving, "section", 1)
    cotangent = shifted_2(returning, "section", -1)
    gain_row = query_gain[0]
    block_table = block_tables[0]
    block_pool = lax.all_gather(prompt_cache, "fork", axis=2, tiled=True)[0]
    fresh_keys, fresh_values = prompt_rows(block_pool, block_table)
    section_output = forward_layer(
        incoming[0, 0], gain_row, fresh_keys, fresh_values, fresh_cache[0, 0], fresh_lengths[0]
    )
    second_pool = lax.all_gather(prompt_cache, "fork", axis=2, tiled=True)[0]
    back_keys, back_values = prompt_rows(second_pool, block_table)
    input_grad, own_grad, shared_grad, gain_part = backward_layer(
        saved_input[0, 0],
        gain_row,
        back_keys,
        back_values,
        back_cache[0, 0],
        back_lengths[0],
        cotangent[0, 0],
    )
    pool_blocks = block_pool.shape[1] // BLOCK
    width = block_pool.shape[2]
    pool_part = jnp.zeros((2, pool_blocks, BLOCK, width), jnp.float32)
    pool_part = pool_part.at[:, block_table].set(
        shared_grad.reshape(2, block_table.shape[0], BLOCK, width)
    )
    pool_part = pool_part.reshape(1, 2, pool_blocks * BLOCK, width)
    prompt_grad = lax.psum_scatter(pool_part, "fork", scatter_dimension=2, tiled=True)
    gain_grad = lax.psum(gain_part, "fork")
    return (
        section_output[None, None],
        input_grad[None, None],
        prompt_grad,
        own_grad[None, None],
        gain_grad[None],
    )


def solution(mesh):
    return jax.shard_map(
        shards,
        mesh=mesh,
        in_specs=(
            P("section", "fork", None, None),
            P("section", "fork", None, None),
            P("section", "fork", None, None),
            P("section", None, "fork", None),
            P("section", "fork", None, None, None),
            P("section", "fork", None, None, None),
            P("section", None),
            P("fork", None),
            P("fork"),
            P("fork"),
        ),
        out_specs=(
            P("section", "fork", None, None),
            P("section", "fork", None, None),
            P("section", None, "fork", None),
            P("section", "fork", None, None, None),
            P("section", None),
        ),
        check_vma=False,
    )
```

profile of v0, /device:TPU:0, one launch (start us, length us, event | category | flops | bytes accessed | tf_op | source)
XLA Modules:
  0.0 209.2 jit_solution(13598215828661033978)
XLA Ops:
  8.0 3.9 %collective-permute-start.1 = (bf16[1,1,128,4096]{3,2,1,0:T(8,128)(2,1)}, bf16[1,1,128,4096]{3,2,1,0:T(8,128)(2,1)}, u32[]{:S(2)}, u32[]{:S(2)}) collective-permute-start(bf16[1,1,128,4096]{3,2,1,0:T(8,128)(2,1)} %param.18), channel_id=1, source_target_pairs={{0,24},{8,0},{16,8},{24,16},{1,25},{9,1},{17,9},{25,17},{2,26},{10... | collective-permute-start | bytes 3145736 | tf_op jit(solution)/shard_map/ppermute | solution.py:18
  11.9 2.0 multiply_reduce_fusion
  15.2 1.6 fusion.95
  23.8 1.0 copy.107
  25.0 1.7 copy.110
  26.7 1.0 copy.81
  27.7 1.3 concatenate.44
  29.0 1.3 concatenate.38
  31.0 1.2 compare_and_fusion
  32.1 1.2 fusion.84
  33.3 1.1 multiply_multiply_fusion
  34.4 1.5 fusion.80
  35.9 1.5 copy.104
  37.4 20.7 %collective-permute-done = bf16[1,1,128,4096]{3,2,1,0:T(8,128)(2,1)} collective-permute-done((bf16[1,1,128,4096]{3,2,1,0:T(8,128)(2,1)}, bf16[1,1,128,4096]{3,2,1,0:T(8,128)(2,1)}, u32[]{:S(2)}, u32[]{:S(2)}) %collective-permute-start) | collective-permute-done | bytes 1048608 | tf_op jit(solution)/shard_map/ppermute | solution.py:18
  58.1 2.6 %copy.102 = f32[1,1,128,4096]{2,3,1,0:T(8,128)} copy(bf16[1,1,128,4096]{3,2,1,0:T(8,128)(2,1)} %collective-permute-done) | data formatting | bytes 3145728 | tf_op jit(solution)/shard_map/convert_element_type | solution.py:22
  60.7 1.5 multiply_reduce_fusion.1
  62.8 1.8 fusion.81
  64.6 1.9 gather_fusion
  67.5 1.1 maximum_bitcast_fusion.4
  68.7 1.1 maximum_bitcast_fusion.5
  69.8 1.4 broadcast.198.clone
  71.3 53.7 %while.25 = (s32[]{:T(128)}, f32[4,128,1024]{1,2,0:T(8,128)}, f32[4,384,128]{2,1,0:T(8,128)}, f32[4,384,128]{2,1,0:T(8,128)}, bf16[4,384,128]{2,1,0:T(8,128)(2,1...) while((s32[]{:T(128)}, f32[4,128,1024]{1,2,0:T(8,128)}, ...), condition=%wide.region_10.12_spmd, body=%wide.region_6.11_spmd.sunk | while | flops 613028352 | bytes 28126012 | solution.py:103
  71.3 1.3 constant_dynamic-slice_fusion.6
  72.7 2.4 %fusion.143 = (f32[8,128]{1,0:T(8,128)}, f32[8,128,384]{1,2,0:T(8,128)}) fusion(bf16[128,8,128]{0,2,1:T(8,128)(2,1)S(1)} %bitcast.254, pred[128,384]{0,1:T(8,128)(4,1)S(1)} %get-tuple-element.312, bf16[4,384,128]{2,1,0:T(8,128)(2,1)S(1)} %get-tuple-element.311, s32[]{:T(128)} %get-tuple-element.297), kind=kOutput, calls=%fused_computation.108.clone.1 | convolution fusion | flops 102236544 | bytes 1986564 | tf_op jit(solution)/shard_map/while/body/eval_jaxpr/sub | solution.py:44
  75.4 3.2 %fusion.145 = f32[4,384,128]{2,1,0:T(8,128)} fusion(f32[4,384,128]{2,1,0:T(8,128)} %get-tuple-element.299, s32[]{:T(128)} %get-tuple-element.297, bf16[128,8,128]{0,2,1:T(8,128)(2,1)S(1)} %bitcast.255, f32[384,128,8]{1,0,2:T(8,128)S(1)} %fusion.142, f32[8,128,384]{1,2,0:T(8,128)} %get-tuple-element.285, f32[8,128]{1,0:T(8,128)} %get-tuple-element.286), kind=kOutput, calls=%fused_computation.38.clone.1 | convolution fusion | flops 103417216 | bytes 6758912 | tf_op jit(solution)/shard_map/while/body/eval_jaxpr/hit,ihd->td/dot_general | solution.py:100
  78.6 2.5 %fusion.144 = f32[128,8,128]{2,0,1:T(8,128)S(1)} fusion(f32[384,128,8]{1,0,2:T(8,128)S(1)} %fusion.142, bf16[4,384,128]{2,1,0:T(8,128)(2,1)} %copy-done.13, s32[]{:T(128)} %get-tuple-element.297, f32[8,128,384]{1,2,0:T(8,128)} %get-tuple-element.285, f32[8,128]{1,0:T(8,128)S(1)} %copy-done.28), kind=kOutput, calls=%fused_computation.39.clone.1 | convolution fusion | flops 103417216 | bytes 6922752 | tf_op jit(solution)/shard_map/while/body/eval_jaxpr/hit,td->ihd/dot_general | solution.py:97
  82.0 2.7 %fusion.146 = f32[4,384,128]{2,1,0:T(8,128)} fusion(f32[4,384,128]{2,1,0:T(8,128)} %get-tuple-element.300, s32[]{:T(128)} %get-tuple-element.297, bf16[128,8,128]{0,2,1:T(8,128)(2,1)S(1)} %bitcast.243, f32[8,128]{1,0:T(8,128)} %get-tuple-element.286, bf16[128,8,128]{0,2,1:T(8,128)(2,1)} %bitcast.256, pred[128,384]{0,1:T(8,128)(4,1)} %get-tuple-element.353, ...), kind=kOutput, calls=%fused_computation.36.clone.1 | convolution fusion | flops 203294080 | bytes 873472 | tf_op jit(solution)/shard_map/while/body/eval_jaxpr/hit,ihd->td/dot_general | solution.py:93
  84.7 1.3 constant_dynamic-slice_fusion.6
  86.1 2.4 %fusion.143 = (f32[8,128]{1,0:T(8,128)}, f32[8,128,384]{1,2,0:T(8,128)}) fusion(bf16[128,8,128]{0,2,1:T(8,128)(2,1)S(1)} %bitcast.254, pred[128,384]{0,1:T(8,128)(4,1)S(1)} %get-tuple-element.312, bf16[4,384,128]{2,1,0:T(8,128)(2,1)S(1)} %get-tuple-element.311, s32[]{:T(128)} %get-tuple-element.297), kind=kOutput, calls=%fused_computation.108.clone.1 | convolution fusion | flops 102236544 | bytes 1986564 | tf_op jit(solution)/shard_map/while/body/eval_jaxpr/sub | solution.py:44
  88.8 3.2 %fusion.145 = f32[4,384,128]{2,1,0:T(8,128)} fusion(f32[4,384,128]{2,1,0:T(8,128)} %get-tuple-element.299, s32[]{:T(128)} %get-tuple-element.297, bf16[128,8,128]{0,2,1:T(8,128)(2,1)S(1)} %bitcast.255, f32[384,128,8]{1,0,2:T(8,128)S(1)} %fusion.142, f32[8,128,384]{1,2,0:T(8,128)} %get-tuple-element.285, f32[8,128]{1,0:T(8,128)} %get-tuple-element.286), kind=kOutput, calls=%fused_computation.38.clone.1 | convolution fusion | flops 103417216 | bytes 6758912 | tf_op jit(solution)/shard_map/while/body/eval_jaxpr/hit,ihd->td/dot_general | solution.py:100
  92.0 2.5 %fusion.144 = f32[128,8,128]{2,0,1:T(8,128)S(1)} fusion(f32[384,128,8]{1,0,2:T(8,128)S(1)} %fusion.142, bf16[4,384,128]{2,1,0:T(8,128)(2,1)} %copy-done.13, s32[]{:T(128)} %get-tuple-element.297, f32[8,128,384]{1,2,0:T(8,128)} %get-tuple-element.285, f32[8,128]{1,0:T(8,128)S(1)} %copy-done.28), kind=kOutput, calls=%fused_computation.39.clone.1 | convolution fusion | flops 103417216 | bytes 6922752 | tf_op jit(solution)/shard_map/while/body/eval_jaxpr/hit,td->ihd/dot_general | solution.py:97
  95.4 2.7 %fusion.146 = f32[4,384,128]{2,1,0:T(8,128)} fusion(f32[4,384,128]{2,1,0:T(8,128)} %get-tuple-element.300, s32[]{:T(128)} %get-tuple-element.297, bf16[128,8,128]{0,2,1:T(8,128)(2,1)S(1)} %bitcast.243, f32[8,128]{1,0:T(8,128)} %get-tuple-element.286, bf16[128,8,128]{0,2,1:T(8,128)(2,1)} %bitcast.256, pred[128,384]{0,1:T(8,128)(4,1)} %get-tuple-element.353, ...), kind=kOutput, calls=%fused_computation.36.clone.1 | convolution fusion | flops 203294080 | bytes 873472 | tf_op jit(solution)/shard_map/while/body/eval_jaxpr/hit,ihd->td/dot_general | solution.py:93
  98.2 1.3 constant_dynamic-slice_fusion.6
  99.5 2.4 %fusion.143 = (f32[8,128]{1,0:T(8,128)}, f32[8,128,384]{1,2,0:T(8,128)}) fusion(bf16[128,8,128]{0,2,1:T(8,128)(2,1)S(1)} %bitcast.254, pred[128,384]{0,1:T(8,128)(4,1)S(1)} %get-tuple-element.312, bf16[4,384,128]{2,1,0:T(8,128)(2,1)S(1)} %get-tuple-element.311, s32[]{:T(128)} %get-tuple-element.297), kind=kOutput, calls=%fused_computation.108.clone.1 | convolution fusion | flops 102236544 | bytes 1986564 | tf_op jit(solution)/shard_map/while/body/eval_jaxpr/sub | solution.py:44
  102.3 3.2 %fusion.145 = f32[4,384,128]{2,1,0:T(8,128)} fusion(f32[4,384,128]{2,1,0:T(8,128)} %get-tuple-element.299, s32[]{:T(128)} %get-tuple-element.297, bf16[128,8,128]{0,2,1:T(8,128)(2,1)S(1)} %bitcast.255, f32[384,128,8]{1,0,2:T(8,128)S(1)} %fusion.142, f32[8,128,384]{1,2,0:T(8,128)} %get-tuple-element.285, f32[8,128]{1,0:T(8,128)} %get-tuple-element.286), kind=kOutput, calls=%fused_computation.38.clone.1 | convolution fusion | flops 103417216 | bytes 6758912 | tf_op jit(solution)/shard_map/while/body/eval_jaxpr/hit,ihd->td/dot_general | solution.py:100
  105.5 2.5 %fusion.144 = f32[128,8,128]{2,0,1:T(8,128)S(1)} fusion(f32[384,128,8]{1,0,2:T(8,128)S(1)} %fusion.142, bf16[4,384,128]{2,1,0:T(8,128)(2,1)} %copy-done.13, s32[]{:T(128)} %get-tuple-element.297, f32[8,128,384]{1,2,0:T(8,128)} %get-tuple-element.285, f32[8,128]{1,0:T(8,128)S(1)} %copy-done.28), kind=kOutput, calls=%fused_computation.39.clone.1 | convolution fusion | flops 103417216 | bytes 6922752 | tf_op jit(solution)/shard_map/while/body/eval_jaxpr/hit,td->ihd/dot_general | solution.py:97
  108.9 2.7 %fusion.146 = f32[4,384,128]{2,1,0:T(8,128)} fusion(f32[4,384,128]{2,1,0:T(8,128)} %get-tuple-element.300, s32[]{:T(128)} %get-tuple-element.297, bf16[128,8,128]{0,2,1:T(8,128)(2,1)S(1)} %bitcast.243, f32[8,128]{1,0:T(8,128)} %get-tuple-element.286, bf16[128,8,128]{0,2,1:T(8,128)(2,1)} %bitcast.256, pred[128,384]{0,1:T(8,128)(4,1)} %get-tuple-element.353, ...), kind=kOutput, calls=%fused_computation.36.clone.1 | convolution fusion | flops 203294080 | bytes 873472 | tf_op jit(solution)/shard_map/while/body/eval_jaxpr/hit,ihd->td/dot_general | solution.py:93
  111.6 1.3 constant_dynamic-slice_fusion.6
  113.0 2.4 %fusion.143 = (f32[8,128]{1,0:T(8,128)}, f32[8,128,384]{1,2,0:T(8,128)}) fusion(bf16[128,8,128]{0,2,1:T(8,128)(2,1)S(1)} %bitcast.254, pred[128,384]{0,1:T(8,128)(4,1)S(1)} %get-tuple-element.312, bf16[4,384,128]{2,1,0:T(8,128)(2,1)S(1)} %get-tuple-element.311, s32[]{:T(128)} %get-tuple-element.297), kind=kOutput, calls=%fused_computation.108.clone.1 | convolution fusion | flops 102236544 | bytes 1986564 | tf_op jit(solution)/shard_map/while/body/eval_jaxpr/sub | solution.py:44
  115.7 3.2 %fusion.145 = f32[4,384,128]{2,1,0:T(8,128)} fusion(f32[4,384,128]{2,1,0:T(8,128)} %get-tuple-element.299, s32[]{:T(128)} %get-tuple-element.297, bf16[128,8,128]{0,2,1:T(8,128)(2,1)S(1)} %bitcast.255, f32[384,128,8]{1,0,2:T(8,128)S(1)} %fusion.142, f32[8,128,384]{1,2,0:T(8,128)} %get-tuple-element.285, f32[8,128]{1,0:T(8,128)} %get-tuple-element.286), kind=kOutput, calls=%fused_computation.38.clone.1 | convolution fusion | flops 103417216 | bytes 6758912 | tf_op jit(solution)/shard_map/while/body/eval_jaxpr/hit,ihd->td/dot_general | solution.py:100
  119.0 2.5 %fusion.144 = f32[128,8,128]{2,0,1:T(8,128)S(1)} fusion(f32[384,128,8]{1,0,2:T(8,128)S(1)} %fusion.142, bf16[4,384,128]{2,1,0:T(8,128)(2,1)} %copy-done.13, s32[]{:T(128)} %get-tuple-element.297, f32[8,128,384]{1,2,0:T(8,128)} %get-tuple-element.285, f32[8,128]{1,0:T(8,128)S(1)} %copy-done.28), kind=kOutput, calls=%fused_computation.39.clone.1 | convolution fusion | flops 103417216 | bytes 6922752 | tf_op jit(solution)/shard_map/while/body/eval_jaxpr/hit,td->ihd/dot_general | solution.py:97
  122.3 2.7 %fusion.146 = f32[4,384,128]{2,1,0:T(8,128)} fusion(f32[4,384,128]{2,1,0:T(8,128)} %get-tuple-element.300, s32[]{:T(128)} %get-tuple-element.297, bf16[128,8,128]{0,2,1:T(8,128)(2,1)S(1)} %bitcast.243, f32[8,128]{1,0:T(8,128)} %get-tuple-element.286, bf16[128,8,128]{0,2,1:T(8,128)(2,1)} %bitcast.256, pred[128,384]{0,1:T(8,128)(4,1)} %get-tuple-element.353, ...), kind=kOutput, calls=%fused_computation.36.clone.1 | convolution fusion | flops 203294080 | bytes 873472 | tf_op jit(solution)/shard_map/while/body/eval_jaxpr/hit,ihd->td/dot_general | solution.py:93
  125.0 1.2 slice.56
  127.6 1.6 broadcast_in_dim.73
  129.1 3.0 %scatter_fusion = f32[2,32,16,512]{3,2,1,0:T(8,128)} fusion(f32[2,32,16,512]{3,2,1,0:T(8,128)} %broadcast_in_dim.73, s32[16]{0:T(128)S(1)} %copy-done.25, f32[16,2,16,512]{3,2,1,0:T(8,128)S(1)} %copy.89), kind=kCustom, calls=%fused_computation.1 | custom fusion | bytes 3145792 | tf_op jit(solution)/shard_map/scatter | solution.py:155
  132.2 1.6 copy-done.1
  133.7 4.3 %fusion.76 = (f32[4,1024]{1,0:T(4,128)}, f32[128]{0:T(128)}, bf16[4,128,1024]{1,2,0:T(8,128)(2,1)}) fusion(f32[128,4,1024]{0,2,1:T(8,128)S(1)} %bitcast.245, f32[4,128,1024]{1,2,0:T(8,128)} %get-tuple-element.344, f32[128]{0:T(128)} %copy-done.22, f32[4,1024]{1,0:T(4,128)S(1)} %mul.161, f32[128,4,1024]{0,2,1:T(8,128)} %bitcast.251, f32[128]{0:T(128)} %add_rsqrt_fusion.1), kind=kLoop, calls=%fused_computation.71 | loop fusion | flops 4714368 | bytes 7374336 | tf_op jit(solution)/shard_map/reduce_sum | solution.py:114
  138.0 1.7 slice.58
  139.8 1.7 slice.59
  141.8 1.5 broadcast.198
  143.3 13.4 %while.24 = (s32[]{:T(128)}, f32[4,128,1024]{1,2,0:T(8,128)}, bf16[4,384,128]{1,2,0:T(8,128)(2,1)S(1)}, pred[128,384]{0,1:T(8,128)(4,1)S(1)}, bf16[4,384,128]{2,...) while((s32[]{:T(128)}, f32[4,128,1024]{1,2,0:T(8,128)}, bf16[4,384,128]{1,2,0:T(8,128)(2,1)S(1)}, ...), condition=%wide.region_4.6_spmd, body=%wide.region_1.5_spmd.sunk | while | flops 305530624 | bytes 3024469 | solution.py:69
  143.3 1.0 constant_dynamic-slice_fusion.5
  146.7 1.0 constant_dynamic-slice_fusion.5
  150.0 1.0 constant_dynamic-slice_fusion.5
  151.6 0.9 fusion.131
  153.4 1.0 constant_dynamic-slice_fusion.5
  156.7 3.1 %copy.103 = f32[1,1,128,4096]{3,2,1,0:T(8,128)} copy(f32[1,1,128,4096]{2,3,1,0:T(8,128)} %bitcast.250) | data formatting | bytes 4194304 | tf_op jit(solution)/shard_map/reshape | solution.py:72
  159.8 1.8 copy.105
  161.7 2.0 copy.90
  163.7 1.8 stack.21
  166.3 1.1 stack.22
  167.4 28.6 %psum.7 = f32[1,4096]{1,0:T(1,128)} all-reduce(f32[1,4096]{1,0:T(1,128)S(1)} %bitcast.267), channel_id=1, replica_groups=mesh['section'=4,'fork'=8] {'fork'}, use_global_device_ids=true, to_apply=%region_15.17 | all-reduce | flops 4096 | bytes 32768 | tf_op jit(solution)/shard_map/psum | solution.py:160
  196.0 1.8 maximum_bitcast_fusion.1
  197.8 4.6 %add_convert_fusion = (bf16[1,1,128,4096]{3,2,1,0:T(8,128)(2,1)}, bf16[1,1,128,4096]{3,2,1,0:T(8,128)(2,1)}) fusion(f32[1,1,128,4096]{3,2,1,0:T(8,128)} %copy.105, f32[128]{0:T(128)S(1)} %broadcast_multiply_fusion, f32[128]{0:T(128)S(1)} %copy-done.27, f32[4096]{0:T(1024)S(1)} %bitcast.268, f32[128]{0:T(128)S(1)} %copy-done.23, ...), kind=kLoop, calls=%fused_computation.74 | loop fusion | flops 6815744 | bytes 9455616 | tf_op jit(solution)/shard_map/convert_element_type | solution.py:117
  (165 shorter events, 26.1 us)
Async XLA Ops:
  7.2 13.6 %copy-start.3 = (bf16[1,1,128,4096]{3,2,1,0:T(8,128)(2,1)S(1)}, bf16[1,1,128,4096]{3,2,1,0:T(8,128)(2,1)}, u32[]{:S(2)}) copy-start(bf16[1,1,128,4096]{3,2,1,0:T(8,128)(2,1)} %param.17) | copy-start | bytes 3145732
  7.2 9.6 %copy-start.15 = (bf16[1,1,2,128,512]{4,3,2,1,0:T(8,128)(2,1)S(1)}, bf16[1,1,2,128,512]{4,3,2,1,0:T(8,128)(2,1)}, u32[]{:S(2)}) copy-start(bf16[1,1,2,128,512]{4,3,2,1,0:T(8,128)(2,1)} %param.21) | copy-start | bytes 786436
  7.2 57.4 %all-gather.2.cloned.1.call-start = ((), (), s32[]{:S(2)}) async-start(), calls=%async_computation.1 | async-start | bytes 1179648 | tf_op jit(solution)/shard_map/all_gather | solution.py:136
  7.9 194.5 %reduce-scatter.2.cloned.1.call-start = ((), (), s32[]{:S(2)}) async-start(), calls=%async_computation.2 | async-start | bytes 2359296 | tf_op jit(solution)/shard_map/reduce_scatter | solution.py:159
  8.0 27.9 %collective-permute-start.1 = (bf16[1,1,128,4096]{3,2,1,0:T(8,128)(2,1)}, bf16[1,1,128,4096]{3,2,1,0:T(8,128)(2,1)}, u32[]{:S(2)}, u32[]{:S(2)}) collective-permute-start(bf16[1,1,128,4096]{3,2,1,0:T(8,128)(2,1)} %param.18), channel_id=1, source_target_pairs={{0,24},{8,0},{16,8},{24,16},{1,25},{9,1},{17,9},{25,17},{2,26},{10... | collective-permute-start | bytes 3145736 | tf_op jit(solution)/shard_map/ppermute | solution.py:18
  11.9 46.2 %collective-permute-start = (bf16[1,1,128,4096]{3,2,1,0:T(8,128)(2,1)}, bf16[1,1,128,4096]{3,2,1,0:T(8,128)(2,1)}, u32[]{:S(2)}, u32[]{:S(2)}) collective-permute-start(bf16[1,1,128,4096]{3,2,1,0:T(8,128)(2,1)} %param.16), channel_id=1, source_target_pairs={{0,8},{8,16},{16,24},{24,0},{1,9},{9,17},{17,25},{25,1},{2,10},{10... | collective-permute-start | bytes 3145736 | tf_op jit(solution)/shard_map/ppermute | solution.py:18
  20.8 1.1 copy-start.17
  21.3 14.6 %copy-start = (f32[1,1,128,4096]{2,3,1,0:T(8,128)}, f32[1,1,128,4096]{2,3,1,0:T(8,128)S(1)}, u32[]{:S(2)}) copy-start(f32[1,1,128,4096]{2,3,1,0:T(8,128)S(1)} %copy.106) | copy-start | bytes 6291460
  34.4 1.5 copy-start.22
  66.5 0.9 copy-start.12
  69.8 1.5 copy-start.20
  71.3 3.7 %copy-start.13 = (bf16[4,384,128]{2,1,0:T(8,128)(2,1)}, bf16[4,384,128]{2,1,0:T(8,128)(2,1)S(1)}, u32[]{:S(2)}) copy-start(bf16[4,384,128]{2,1,0:T(8,128)(2,1)S(1)} %get-tuple-element.311) | copy-start | bytes 1179652 | tf_op jit(solution)/shard_map/while
  71.3 3.7 %copy-start.6 = (bf16[4,384,128]{2,1,0:T(8,128)(2,1)}, bf16[4,384,128]{2,1,0:T(8,128)(2,1)S(1)}, u32[]{:S(2)}) copy-start(bf16[4,384,128]{2,1,0:T(8,128)(2,1)S(1)} %get-tuple-element.314) | copy-start | bytes 1179652 | tf_op jit(solution)/shard_map/while
  72.7 2.7 %copy-start.5 = (bf16[1,128,1024]{1,2,0:T(8,128)(2,1)}, bf16[1,128,1024]{1,2,0:T(8,128)(2,1)S(1)}, u32[]{:S(2)}) copy-start(bf16[1,128,1024]{1,2,0:T(8,128)(2,1)S(1)} %get-tuple-element.284) | copy-start | bytes 786436 | tf_op jit(solution)/shard_map/while
  75.4 3.2 %copy-start.28 = (f32[8,128]{1,0:T(8,128)S(1)}, f32[8,128]{1,0:T(8,128)}, u32[]{:S(2)}) copy-start(f32[8,128]{1,0:T(8,128)} %get-tuple-element.286) | copy-start | bytes 12292 | tf_op jit(solution)/shard_map/while
  82.0 2.7 %copy-start.7 = (bf16[4,384,128]{2,1,0:T(8,128)(2,1)S(1)}, bf16[4,384,128]{2,1,0:T(8,128)(2,1)}, u32[]{:S(2)}) copy-start(bf16[4,384,128]{2,1,0:T(8,128)(2,1)} %copy-done.6) | copy-start | bytes 1179652 | tf_op jit(solution)/shard_map/while
  82.0 2.7 %copy-start.14 = (bf16[4,384,128]{2,1,0:T(8,128)(2,1)S(1)}, bf16[4,384,128]{2,1,0:T(8,128)(2,1)}, u32[]{:S(2)}) copy-start(bf16[4,384,128]{2,1,0:T(8,128)(2,1)} %copy-done.13) | copy-start | bytes 1179652 | tf_op jit(solution)/shard_map/while
  82.0 2.7 %copy-start.21 = (pred[128,384]{0,1:T(8,128)(4,1)S(1)}, pred[128,384]{0,1:T(8,128)(4,1)}, u32[]{:S(2)}) copy-start(pred[128,384]{0,1:T(8,128)(4,1)} %get-tuple-element.353) | copy-start | bytes 147460 | tf_op jit(solution)/shard_map/while
  84.7 3.8 %copy-start.13 = (bf16[4,384,128]{2,1,0:T(8,128)(2,1)}, bf16[4,384,128]{2,1,0:T(8,128)(2,1)S(1)}, u32[]{:S(2)}) copy-start(bf16[4,384,128]{2,1,0:T(8,128)(2,1)S(1)} %get-tuple-element.311) | copy-start | bytes 1179652 | tf_op jit(solution)/shard_map/while
  84.7 3.7 %copy-start.6 = (bf16[4,384,128]{2,1,0:T(8,128)(2,1)}, bf16[4,384,128]{2,1,0:T(8,128)(2,1)S(1)}, u32[]{:S(2)}) copy-start(bf16[4,384,128]{2,1,0:T(8,128)(2,1)S(1)} %get-tuple-element.314) | copy-start | bytes 1179652 | tf_op jit(solution)/shard_map/while
  86.1 2.7 %copy-start.5 = (bf16[1,128,1024]{1,2,0:T(8,128)(2,1)}, bf16[1,128,1024]{1,2,0:T(8,128)(2,1)S(1)}, u32[]{:S(2)}) copy-start(bf16[1,128,1024]{1,2,0:T(8,128)(2,1)S(1)} %get-tuple-element.284) | copy-start | bytes 786436 | tf_op jit(solution)/shard_map/while
  88.8 3.2 %copy-start.28 = (f32[8,128]{1,0:T(8,128)S(1)}, f32[8,128]{1,0:T(8,128)}, u32[]{:S(2)}) copy-start(f32[8,128]{1,0:T(8,128)} %get-tuple-element.286) | copy-start | bytes 12292 | tf_op jit(solution)/shard_map/while
  95.4 2.7 %copy-start.7 = (bf16[4,384,128]{2,1,0:T(8,128)(2,1)S(1)}, bf16[4,384,128]{2,1,0:T(8,128)(2,1)}, u32[]{:S(2)}) copy-start(bf16[4,384,128]{2,1,0:T(8,128)(2,1)} %copy-done.6) | copy-start | bytes 1179652 | tf_op jit(solution)/shard_map/while
  95.4 2.7 %copy-start.14 = (bf16[4,384,128]{2,1,0:T(8,128)(2,1)S(1)}, bf16[4,384,128]{2,1,0:T(8,128)(2,1)}, u32[]{:S(2)}) copy-start(bf16[4,384,128]{2,1,0:T(8,128)(2,1)} %copy-done.13) | copy-start | bytes 1179652 | tf_op jit(solution)/shard_map/while
  95.4 2.7 %copy-start.21 = (pred[128,384]{0,1:T(8,128)(4,1)S(1)}, pred[128,384]{0,1:T(8,128)(4,1)}, u32[]{:S(2)}) copy-start(pred[128,384]{0,1:T(8,128)(4,1)} %get-tuple-element.353) | copy-start | bytes 147460 | tf_op jit(solution)/shard_map/while
  98.1 3.8 %copy-start.13 = (bf16[4,384,128]{2,1,0:T(8,128)(2,1)}, bf16[4,384,128]{2,1,0:T(8,128)(2,1)S(1)}, u32[]{:S(2)}) copy-start(bf16[4,384,128]{2,1,0:T(8,128)(2,1)S(1)} %get-tuple-element.311) | copy-start | bytes 1179652 | tf_op jit(solution)/shard_map/while
  98.2 3.7 %copy-start.6 = (bf16[4,384,128]{2,1,0:T(8,128)(2,1)}, bf16[4,384,128]{2,1,0:T(8,128)(2,1)S(1)}, u32[]{:S(2)}) copy-start(bf16[4,384,128]{2,1,0:T(8,128)(2,1)S(1)} %get-tuple-element.314) | copy-start | bytes 1179652 | tf_op jit(solution)/shard_map/while
  99.5 2.7 %copy-start.5 = (bf16[1,128,1024]{1,2,0:T(8,128)(2,1)}, bf16[1,128,1024]{1,2,0:T(8,128)(2,1)S(1)}, u32[]{:S(2)}) copy-start(bf16[1,128,1024]{1,2,0:T(8,128)(2,1)S(1)} %get-tuple-element.284) | copy-start | bytes 786436 | tf_op jit(solution)/shard_map/while
  102.3 3.2 %copy-start.28 = (f32[8,128]{1,0:T(8,128)S(1)}, f32[8,128]{1,0:T(8,128)}, u32[]{:S(2)}) copy-start(f32[8,128]{1,0:T(8,128)} %get-tuple-element.286) | copy-start | bytes 12292 | tf_op jit(solution)/shard_map/while
  108.9 2.7 %copy-start.7 = (bf16[4,384,128]{2,1,0:T(8,128)(2,1)S(1)}, bf16[4,384,128]{2,1,0:T(8,128)(2,1)}, u32[]{:S(2)}) copy-start(bf16[4,384,128]{2,1,0:T(8,128)(2,1)} %copy-done.6) | copy-start | bytes 1179652 | tf_op jit(solution)/shard_map/while
  108.9 2.7 %copy-start.14 = (bf16[4,384,128]{2,1,0:T(8,128)(2,1)S(1)}, bf16[4,384,128]{2,1,0:T(8,128)(2,1)}, u32[]{:S(2)}) copy-start(bf16[4,384,128]{2,1,0:T(8,128)(2,1)} %copy-done.13) | copy-start | bytes 1179652 | tf_op jit(solution)/shard_map/while
  108.9 2.7 %copy-start.21 = (pred[128,384]{0,1:T(8,128)(4,1)S(1)}, pred[128,384]{0,1:T(8,128)(4,1)}, u32[]{:S(2)}) copy-start(pred[128,384]{0,1:T(8,128)(4,1)} %get-tuple-element.353) | copy-start | bytes 147460 | tf_op jit(solution)/shard_map/while
  111.6 3.8 %copy-start.13 = (bf16[4,384,128]{2,1,0:T(8,128)(2,1)}, bf16[4,384,128]{2,1,0:T(8,128)(2,1)S(1)}, u32[]{:S(2)}) copy-start(bf16[4,384,128]{2,1,0:T(8,128)(2,1)S(1)} %get-tuple-element.311) | copy-start | bytes 1179652 | tf_op jit(solution)/shard_map/while
  111.6 3.7 %copy-start.6 = (bf16[4,384,128]{2,1,0:T(8,128)(2,1)}, bf16[4,384,128]{2,1,0:T(8,128)(2,1)S(1)}, u32[]{:S(2)}) copy-start(bf16[4,384,128]{2,1,0:T(8,128)(2,1)S(1)} %get-tuple-element.314) | copy-start | bytes 1179652 | tf_op jit(solution)/shard_map/while
  113.0 2.7 %copy-start.5 = (bf16[1,128,1024]{1,2,0:T(8,128)(2,1)}, bf16[1,128,1024]{1,2,0:T(8,128)(2,1)S(1)}, u32[]{:S(2)}) copy-start(bf16[1,128,1024]{1,2,0:T(8,128)(2,1)S(1)} %get-tuple-element.284) | copy-start | bytes 786436 | tf_op jit(solution)/shard_map/while
  115.7 3.2 %copy-start.28 = (f32[8,128]{1,0:T(8,128)S(1)}, f32[8,128]{1,0:T(8,128)}, u32[]{:S(2)}) copy-start(f32[8,128]{1,0:T(8,128)} %get-tuple-element.286) | copy-start | bytes 12292 | tf_op jit(solution)/shard_map/while
  122.3 2.7 %copy-start.7 = (bf16[4,384,128]{2,1,0:T(8,128)(2,1)S(1)}, bf16[4,384,128]{2,1,0:T(8,128)(2,1)}, u32[]{:S(2)}) copy-start(bf16[4,384,128]{2,1,0:T(8,128)(2,1)} %copy-done.6) | copy-start | bytes 1179652 | tf_op jit(solution)/shard_map/while
  122.3 2.7 %copy-start.14 = (bf16[4,384,128]{2,1,0:T(8,128)(2,1)S(1)}, bf16[4,384,128]{2,1,0:T(8,128)(2,1)}, u32[]{:S(2)}) copy-start(bf16[4,384,128]{2,1,0:T(8,128)(2,1)} %copy-done.13) | copy-start | bytes 1179652 | tf_op jit(solution)/shard_map/while
  122.3 2.7 %copy-start.21 = (pred[128,384]{0,1:T(8,128)(4,1)S(1)}, pred[128,384]{0,1:T(8,128)(4,1)}, u32[]{:S(2)}) copy-start(pred[128,384]{0,1:T(8,128)(4,1)} %get-tuple-element.353) | copy-start | bytes 147460 | tf_op jit(solution)/shard_map/while
  125.0 1.7 copy-start.11
  127.6 1.6 copy-start.25
  132.1 1.6 copy-start.1
  133.7 7.7 %copy-start.9 = (bf16[4,384,128]{2,0,1:T(4,128)(2,1)S(1)}, bf16[4,384,128]{2,0,1:T(4,128)(2,1)}, u32[]{:S(2)}) copy-start(bf16[4,384,128]{2,0,1:T(4,128)(2,1)} %get-tuple-element.175) | copy-start | bytes 1179652
  138.0 3.7 %copy-start.8 = (bf16[4,384,128]{2,0,1:T(4,128)(2,1)S(1)}, bf16[4,384,128]{2,0,1:T(4,128)(2,1)}, u32[]{:S(2)}) copy-start(bf16[4,384,128]{2,0,1:T(4,128)(2,1)} %get-tuple-element.179) | copy-start | bytes 1179652
  141.7 1.6 copy-start.19
  156.7 3.1 %copy-start.2 = (f32[4,128,1024]{1,2,0:T(8,128)S(1)}, f32[4,128,1024]{1,2,0:T(8,128)}, u32[]{:S(2)}) copy-start(f32[4,128,1024]{1,2,0:T(8,128)} %get-tuple-element.344) | copy-start | bytes 6291460
  159.8 5.6 %copy-start.10 = (f32[128,4,128]{2,0,1:T(8,128)S(1)}, f32[128,4,128]{2,0,1:T(8,128)}, u32[]{:S(2)}) copy-start(f32[128,4,128]{2,0,1:T(8,128)} %slice.59) | copy-start | bytes 786436
  159.8 7.5 %copy-start.16 = (f32[4,1024]{1,0:T(4,128)S(1)}, f32[4,1024]{1,0:T(4,128)}, u32[]{:S(2)}) copy-start(f32[4,1024]{1,0:T(4,128)} %get-tuple-element.136) | copy-start | bytes 49156
  161.7 36.1 %copy-start.24 = (f32[128]{0:T(128)S(1)}, f32[128]{0:T(128)}, u32[]{:S(2)}) copy-start(f32[128]{0:T(128)} %get-tuple-element.137) | copy-start | bytes 1540
  161.7 36.1 %copy-start.4 = (f32[1,1,128,4096]{3,2,1,0:T(8,128)S(1)}, f32[1,1,128,4096]{3,2,1,0:T(8,128)}, u32[]{:S(2)}) copy-start(f32[1,1,128,4096]{3,2,1,0:T(8,128)} %copy.103) | copy-start | bytes 6291460
  161.7 36.1 %copy-start.18 = (f32[1,4096]{1,0:T(1,128)S(1)}, f32[1,4096]{1,0:T(1,128)}, u32[]{:S(2)}) copy-start(f32[1,4096]{1,0:T(1,128)} %param.22) | copy-start | bytes 49156
  161.7 36.1 %copy-start.23 = (f32[128]{0:T(128)S(1)}, f32[128]{0:T(128)}, u32[]{:S(2)}) copy-start(f32[128]{0:T(128)} %copy-done.22) | copy-start | bytes 1540
  161.7 36.1 %copy-start.26 = (f32[128]{0:T(128)S(1)}, f32[128]{0:T(128)}, u32[]{:S(2)}) copy-start(f32[128]{0:T(128)} %fusion.85) | copy-start | bytes 1540
  161.7 36.1 %copy-start.27 = (f32[128]{0:T(128)S(1)}, f32[128]{0:T(128)}, u32[]{:S(2)}) copy-start(f32[128]{0:T(128)} %get-tuple-element.183) | copy-start | bytes 1540
Sparse Core Ops, SparseCore 0:
  9.6 24.8 all-gather.1
  132.3 36.0 reduce-scatter.1
where the time goes:
time: 211 us; the launch traced here: 209 us
  local copies, waits for them, and re-layouts  59.4 us (28%)
  matrix products  50.7 us (24%)
  other arithmetic  29 us (14%)
  blocking collectives  28.6 us (14%)
  waiting for transfers between devices  21.5 us (10%)
  between operations  15.8 us (7%)
  starting transfers between devices  4.02 us (2%)
    psum x1, blocking collectives, shards(): gain_grad = lax.psum(gain_part, 'fork')  28.6 us
    ppermute x2, waiting for transfers between devices, shifted_2(): return lax.ppermute(value, axis, pairs)  20.8 us
    dot_general x4, matrix products, backward_per_group(): jnp.einsum('hit,ihd->td', d_score, head_rows, preferred_element_type=jnp....  12.8 us
    sub x8, matrix products, softmax_rows(): shifted = jnp.exp(scores - jnp.max(scores, axis=-1, keepdims=True))  12 us
    dot_general x4, matrix products, backward_per_group(): jnp.einsum('hit,ihd->td', rounded, d_out, preferred_element_type=jnp.floa...  10.8 us
    dot_general x4, matrix products, backward_per_group(): jnp.einsum('hit,td->ihd', d_score, k_group, preferred_element_type=jnp.fl...  10.1 us
    dynamic_slice x8, local copies, waits for them, and re-layouts, forward_layer(): lax.map(forward_per_group, (by_group(queries), by_group(all_keys), by_gro...  9.27 us
    dynamic_update_slice x8, local copies, waits for them, and re-layouts, forward_layer(): lax.map(forward_per_group, (by_group(queries), by_group(all_keys), by_gro...  6.72 us
  transfers between devices with their start and end apart: 4, of which 1 were waited for; matrix products, arithmetic and copies ran while one was open for 34% of the time, Pallas kernels for 0%

commit v1 on v0

v1 whole, which is shorter than its diff:
```python
import math

import jax
import jax.numpy as jnp
from jax import lax
from jax.experimental import pallas as pl
from jax.experimental.pallas import tpu as pltpu
from jax.sharding import PartitionSpec as P

KV = 4
HD = 128
BLOCK = 16


epsilon = 1e-06
masked_score = -1e30
scale = HD ** (-0.5)
exp_scale = scale * math.log2(math.e)
vmem_limit = 48 * 1024 * 1024


def shifted_2(value, axis, steps):
    count = lax.axis_size(axis)
    pairs = [(source, (source + steps) % count) for source in range(count)]
    return lax.ppermute(value, axis, pairs)


def gather_rows(table, pool, own, held, which):
    prompt_count = table.shape[0] * BLOCK

    @pl.loop(0, table.shape[0])
    def _(j):
        source = pl.multiple_of(table[j] * BLOCK, BLOCK)
        target = pl.multiple_of(j * BLOCK, BLOCK)
        held[pl.ds(target, BLOCK), :] = pool[which, pl.ds(source, BLOCK), :]

    held[prompt_count:, :] = own[which]


def norm_rows(x, gain, queries, inverses):
    rows = BLOCK

    @pl.loop(0, x.shape[0] // rows)
    def _(i):
        place = pl.ds(pl.multiple_of(i * rows, rows), rows)
        floated = x[place, :].astype(jnp.float32)
        inverse = lax.rsqrt(jnp.mean(floated * floated, axis=-1, keepdims=True) + epsilon)
        queries[place, :] = (floated * inverse * gain[...]).astype(jnp.bfloat16)
        if inverses is not None:
            inverses[place, :] = jnp.broadcast_to(inverse, (rows, HD))


def dot(a, b, left, right):
    return lax.dot_general(a, b, (((left,), (right,)), ((), ())), preferred_element_type=jnp.float32)


def key_mask(rows, length):
    key = lax.broadcasted_iota(jnp.int32, (rows, rows), 0)
    row = lax.broadcasted_iota(jnp.int32, (rows, rows), 1)
    return (key <= row) & (key < length)


def chances_of(q_head, keys, mask):
    rows = mask.shape[0]
    scores = dot(keys, q_head, 1, 1)
    prompt = scores[:-rows]
    recent = jnp.where(mask, scores[-rows:], masked_score)
    top = jnp.maximum(jnp.max(prompt, axis=0, keepdims=True), jnp.max(recent, axis=0, keepdims=True))
    prompt = jnp.exp2((prompt - top) * exp_scale)
    recent = jnp.exp2((recent - top) * exp_scale)
    total = jnp.sum(prompt, axis=0, keepdims=True) + jnp.sum(recent, axis=0, keepdims=True)
    return jnp.concatenate([prompt, recent], axis=0) * (1.0 / total)


def forward_kernel(table, length, x, gain, pool, own, out, queries, keys, values):
    rows, width = x.shape
    group = width // KV
    gather_rows(table, pool, own, keys, 0)
    gather_rows(table, pool, own, values, 1)
    norm_rows(x, gain, queries, None)
    mask = key_mask(rows, length[0])
    valid = (lax.broadcasted_iota(jnp.int32, (rows, HD), 0) < length[0]).astype(jnp.float32)

    @pl.loop(0, KV)
    def _(g):
        columns = pl.ds(pl.multiple_of(g * HD, HD), HD)
        k_group = keys[:, columns]
        v_group = values[:, columns]
        for h in range(group // HD):
            place = pl.ds(pl.multiple_of(g * group + h * HD, HD), HD)
            chances = chances_of(queries[:, place], k_group, mask)
            attended = dot(v_group, chances.astype(jnp.bfloat16), 0, 0).T
            out[:, place] = (x[:, place].astype(jnp.float32) + valid * attended).astype(out.dtype)


def backward_kernel(
    table, length, x, gain, pool, own, cotangent,
    input_grad, pool_grad, own_grad, gain_grad,
    queries, inverses, keys, values, outs, weights, d_scores, d_queries, d_key, d_value,
):
    rows, width = x.shape
    group = width // KV
    prompt_count = table.shape[0] * BLOCK
    pool_grad[...] = jnp.zeros_like(pool_grad)
    gather_rows(table, pool, own, keys, 0)
    gather_rows(table, pool, own, values, 1)
    norm_rows(x, gain, queries, inverses)
    mask = key_mask(rows, length[0])
    valid = (lax.broadcasted_iota(jnp.int32, (rows, HD), 0) < length[0]).astype(jnp.float32)

    @pl.loop(0, KV)
    def _(g):
        columns = pl.ds(pl.multiple_of(g * HD, HD), HD)
        k_group = keys[:, columns]
        v_group = values[:, columns]
        heads = group // HD
        for h in range(heads):
            place = pl.ds(pl.multiple_of(g * group + h * HD, HD), HD)
            spot = slice(h * HD, (h + 1) * HD)
            q_head = queries[:, place]
            out_grad = (valid * cotangent[:, place].astype(jnp.float32)).astype(jnp.bfloat16)
            outs[spot, :] = out_grad
            chances = chances_of(q_head, k_group, mask)
            weights[:, spot] = chances.astype(jnp.bfloat16)
            d_weight = dot(v_group, out_grad, 1, 1)
            delta = jnp.sum(chances * d_weight, axis=0, keepdims=True)
            d_score = (chances * (d_weight - delta) * scale).astype(jnp.bfloat16)
            d_scores[:, spot] = d_score
            d_queries[:, place] = dot(k_group, d_score, 0, 0).T
        q_all = jnp.concatenate(
            [queries[:, pl.ds(pl.multiple_of(g * group + h * HD, HD), HD)] for h in range(heads)], axis=0
        )
        d_value[...] = dot(weights[...], outs[...], 1, 0)
        d_key[...] = dot(d_scores[...], q_all, 1, 0)
        own_grad[0, :, columns] = d_key[prompt_count:, :]
        own_grad[1, :, columns] = d_value[prompt_count:, :]

        @pl.loop(0, table.shape[0])
        def _(j):
            target = pl.ds(pl.multiple_of(table[j] * BLOCK, BLOCK), BLOCK)
            source = pl.ds(pl.multiple_of(j * BLOCK, BLOCK), BLOCK)
            pool_grad[0, target, columns] = d_key[source, :]
            pool_grad[1, target, columns] = d_value[source, :]

    gain_grad[...] = jnp.zeros_like(gain_grad)

    @pl.loop(0, rows // BLOCK)
    def _(i):
        place = pl.ds(pl.multiple_of(i * BLOCK, BLOCK), BLOCK)
        floated = x[place, :].astype(jnp.float32)
        inverse = inverses[place, 0:1]
        d_query = d_queries[place, :]
        d_normed = d_query * gain[...]
        along = jnp.mean(d_normed * floated, axis=-1, keepdims=True)
        d_input = inverse * d_normed - floated * (inverse * inverse * inverse * along)
        input_grad[place, :] = (cotangent[place, :].astype(jnp.float32) + d_input).astype(input_grad.dtype)
        gain_grad[...] += jnp.sum(d_query * floated * inverse, axis=0, keepdims=True)


def forward(table, length, x, gain, pool, own):
    rows, width = x.shape
    count = table.shape[0] * BLOCK + rows
    vmem = pl.BlockSpec(memory_space=pltpu.VMEM)
    smem = pl.BlockSpec(memory_space=pltpu.SMEM)
    return pl.pallas_call(
        forward_kernel,
        out_shape=jax.ShapeDtypeStruct(x.shape, x.dtype),
        in_specs=[smem, smem] + [vmem] * 4,
        out_specs=vmem,
        scratch_shapes=[
            pltpu.VMEM((rows, width), jnp.bfloat16),
            pltpu.VMEM((count, pool.shape[-1]), jnp.bfloat16),
            pltpu.VMEM((count, pool.shape[-1]), jnp.bfloat16),
        ],
        compiler_params=pltpu.CompilerParams(vmem_limit_bytes=vmem_limit),
        cost_estimate=pl.CostEstimate(
            flops=4 * rows * width * count, bytes_accessed=4 * rows * width, transcendentals=rows * width // HD * count
        ),
        name="forward",
    )(table, length, x, gain, pool, own)


def backward(table, length, x, gain, pool, own, cotangent):
    rows, width = x.shape
    count = table.shape[0] * BLOCK + rows
    group = width // KV
    vmem = pl.BlockSpec(memory_space=pltpu.VMEM)
    smem = pl.BlockSpec(memory_space=pltpu.SMEM)
    return pl.pallas_call(
        backward_kernel,
        out_shape=(
            jax.ShapeDtypeStruct(x.shape, x.dtype),
            jax.ShapeDtypeStruct(pool.shape, jnp.float32),
            jax.ShapeDtypeStruct(own.shape, jnp.float32),
            jax.ShapeDtypeStruct((1, width), jnp.float32),
        ),
        in_specs=[smem, smem] + [vmem] * 5,
        out_specs=(vmem,) * 4,
        scratch_shapes=[
            pltpu.VMEM((rows, width), jnp.bfloat16),
            pltpu.VMEM((rows, HD), jnp.float32),
            pltpu.VMEM((count, pool.shape[-1]), jnp.bfloat16),
            pltpu.VMEM((count, pool.shape[-1]), jnp.bfloat16),
            pltpu.VMEM((rows * group // HD, HD), jnp.bfloat16),
            pltpu.VMEM((count, group), jnp.bfloat16),
            pltpu.VMEM((count, group), jnp.bfloat16),
            pltpu.VMEM((rows, width), jnp.float32),
            pltpu.VMEM((count, HD), jnp.float32),
            pltpu.VMEM((count, HD), jnp.float32),
        ],
        compiler_params=pltpu.CompilerParams(vmem_limit_bytes=vmem_limit),
        cost_estimate=pl.CostEstimate(
            flops=10 * rows * width * count, bytes_accessed=10 * rows * width, transcendentals=rows * width // HD * count
        ),
        name="backward",
    )(table, length, x, gain, pool, own, cotangent)


def shards(
    arriving,
    saved_input,
    returning,
    prompt_cache,
    fresh_cache,
    back_cache,
    query_gain,
    block_tables,
    fresh_lengths,
    back_lengths,
):
    cotangent = shifted_2(returning, "section", -1)
    table = block_tables[0]
    pool = lax.all_gather(prompt_cache, "fork", axis=2, tiled=True)[0]
    arriving, cotangent = lax.optimization_barrier((arriving, cotangent))
    incoming = shifted_2(arriving, "section", 1)
    input_grad, pool_grad, own_grad, gain_part = backward(
        table, back_lengths, saved_input[0, 0], query_gain, pool, back_cache[0, 0], cotangent[0, 0]
    )
    prompt_grad = lax.psum_scatter(pool_grad[None], "fork", scatter_dimension=2, tiled=True)
    gain_parts = lax.all_gather(gain_part, "fork", axis=0, tiled=True)
    section_output = forward(
        table, fresh_lengths, incoming[0, 0], query_gain, pool, fresh_cache[0, 0]
    )
    return (
        section_output[None, None],
        input_grad[None, None],
        prompt_grad,
        own_grad[None, None],
        jnp.sum(gain_parts, axis=0, keepdims=True),
    )


def solution(mesh):
    return jax.shard_map(
        shards,
        mesh=mesh,
        in_specs=(
            P("section", "fork", None, None),
            P("section", "fork", None, None),
            P("section", "fork", None, None),
            P("section", None, "fork", None),
            P("section", "fork", None, None, None),
            P("section", "fork", None, None, None),
            P("section", None),
            P("fork", None),
            P("fork"),
            P("fork"),
        ),
        out_specs=(
            P("section", "fork", None, None),
            P("section", "fork", None, None),
            P("section", None, "fork", None),
            P("section", "fork", None, None, None),
            P("section", None),
        ),
        check_vma=False,
    )
```

time: 211 us -> 106 us (0.50)
  local copies, waits for them, and re-layouts: 59.4 us -> 4.79 us
  matrix products: 50.7 us -> 0 us
  other arithmetic: 29 us -> 0.7 us
  Pallas kernels: 0 us -> 28.1 us
  blocking collectives: 28.6 us -> 14.6 us
  waiting for transfers between devices: 21.5 us -> 35.5 us
  starting transfers between devices: 4.02 us -> 6.4 us
    dot_general x20 -> x0, matrix products: 38.7 us -> none  [the longest x4 12.8 us: backward_per_group(): jnp.einsum('hit,ihd->td', d_score, head_rows, preferred_element_type=jnp....]
    psum x1 -> x0, blocking collectives: 28.6 us -> none  [shards(): gain_grad = lax.psum(gain_part, 'fork')]
    pallas_call x0 -> x2, Pallas kernels: none -> 28.1 us  [the longest x1 21.2 us: backward(): pl.pallas_call(backward_kernel, out_shape=(jax.ShapeDtypeStruct(x.shape,...]
    all_gather x0 -> x1, blocking collectives: none -> 14.6 us  [shards(): gain_parts = lax.all_gather(gain_part, 'fork', axis=0, tiled=True)]
    sub x8 -> x0, matrix products: 12 us -> none  [softmax_rows(): shifted = jnp.exp(scores - jnp.max(scores, axis=-1, keepdims=True))]
    slice x11 -> x0, local copies, waits for them, and re-layouts: 10.5 us -> none  [the longest x4 6.25 us: backward_layer(): own_grad = jnp.stack([d_key[prompt_count:], d_value[prompt_count:]])]
    dynamic_slice x8 -> x0, local copies, waits for them, and re-layouts: 9.27 us -> none  [forward_layer(): lax.map(forward_per_group, (by_group(queries), by_group(all_keys), by_gro...]
    ppermute x2, waiting for transfers between devices: 20.8 us -> 30 us  [shifted_2(): return lax.ppermute(value, axis, pairs)]
  transfers between devices with their start and end apart: 4 -> 4, of which waited for: 1 -> 3; matrix products, arithmetic and copies ran while one was open for 34% -> 1% of each run, Pallas kernels for 0% -> 6%
where the time goes in v1:
time: 106 us; the launch traced here: 105 us
  waiting for transfers between devices  35.5 us (33%)
  Pallas kernels  28.1 us (27%)
  between operations  15.4 us (15%)
  blocking collectives  14.6 us (14%)
  starting transfers between devices  6.4 us (6%)
  local copies, waits for them, and re-layouts  4.79 us (5%)
    ppermute x2, waiting for transfers between devices, shifted_2(): return lax.ppermute(value, axis, pairs)  30 us
    pallas_call x1, Pallas kernels, backward(): pl.pallas_call(backward_kernel, out_shape=(jax.ShapeDtypeStruct(x.shape,...  21.2 us
    all_gather x1, blocking collectives, shards(): gain_parts = lax.all_gather(gain_part, 'fork', axis=0, tiled=True)  14.6 us
    pallas_call x1, Pallas kernels, forward(): pl.pallas_call(forward_kernel, out_shape=jax.ShapeDtypeStruct(x.shape, x....  6.83 us
    ppermute x2, starting transfers between devices, shifted_2(): return lax.ppermute(value, axis, pairs)  6.32 us
    reduce_scatter x1, waiting for transfers between devices, shards(): lax.psum_scatter(pool_grad[None], 'fork', scatter_dimension=2, tiled=True)  4.82 us
    unnamed x18, local copies, waits for them, and re-layouts  4.79 us
  transfers between devices with their start and end apart: 4, of which 3 were waited for; matrix products, arithmetic and copies ran while one was open for 1% of the time, Pallas kernels for 6%

profile of v1, /device:TPU:0, one launch (start us, length us, event | category | flops | bytes accessed | tf_op | source)
XLA Modules:
  0.0 105.5 jit_solution(10437890922963937812)
XLA Ops:
  7.2 0.0 all-gather.3.cloned.1.call-start
  7.2 0.7 all-gather.3.cloned.1.call-update
  7.9 0.0 reduce-scatter.2.cloned.1.call-start
  7.9 3.9 %collective-permute-start = (bf16[1,1,128,4096]{3,2,1,0:T(8,128)(2,1)}, bf16[1,1,128,4096]{3,2,1,0:T(8,128)(2,1)S(1)}, u32[]{:S(2)}, u32[]{:S(2)}) collective-permute-start(bf16[1,1,128,4096]{3,2,1,0:T(8,128)(2,1)} %param.12), channel_id=1, source_target_pairs={{0,24},{8,0},{16,8},{24,16},{1,25},{9,1},{17,9},{25,17},{2,26},{10... | collective-permute-start | bytes 3145736 | tf_op jit(solution)/shard_map/ppermute | solution.py:25
  12.5 22.1 %collective-permute-done = bf16[1,1,128,4096]{3,2,1,0:T(8,128)(2,1)S(1)} collective-permute-done((bf16[1,1,128,4096]{3,2,1,0:T(8,128)(2,1)}, bf16[1,1,128,4096]{3,2,1,0:T(8,128)(2,1)S(1)}, u32[]{:S(2)}, u32[]{:S(2)}) %collective-permute-start) | collective-permute-done | bytes 1048608 | tf_op jit(solution)/shard_map/ppermute | solution.py:25
  34.6 0.0 all-gather.3.cloned.1.call-done
  34.6 0.0 copy-start
  34.6 1.2 %copy-done = bf16[1,2,512,512]{3,2,1,0:T(8,128)(2,1)S(1)} copy-done((bf16[1,2,512,512]{3,2,1,0:T(8,128)(2,1)S(1)}, bf16[1,2,512,512]{3,2,1,0:T(8,128)(2,1)}, u32[]{:S(2)}) %copy-start) | copy-done | bytes 1048600
  35.9 0.0 copy-start.3
  35.9 0.7 copy-done.3
  36.6 0.0 copy-start.5
  36.6 0.7 copy-done.5
  37.2 0.0 copy-start.7
  37.2 1.2 %copy-done.7 = bf16[1,1,128,4096]{3,2,1,0:T(8,128)(2,1)S(1)} copy-done((bf16[1,1,128,4096]{3,2,1,0:T(8,128)(2,1)S(1)}, bf16[1,1,128,4096]{3,2,1,0:T(8,128)(2,1)}, u32[]{:S(2)}) %copy-start.7) | copy-done | bytes 1048600
  38.5 0.0 copy-start.8
  38.5 0.9 copy-done.8
  39.4 21.2 %backward.1 = (bf16[128,4096]{1,0:T(8,128)(2,1)}, f32[2,512,512]{2,1,0:T(8,128)}, f32[2,128,512]{2,1,0:T(8,128)}, f32[1,4096]{1,0:T(1,128)S(1)}) custom-call(s32[16]{0:T(128)S(1)} %bitcast.18, s32[1]{0:T(128)S(6)} %copy.16.length, bf16[128,4096]{1,0:T(8,128)(2,1)S(1)} %bitcast.20, f32[1,4096]{1,0:T(1,128)S(1)} %copy-done.3, ...), custom_call_target="tpu_custom_call" | custom-call | flops 2013265920 | bytes 5242880 | tf_op jit(solution)/shard_map/backward/pallas_call | solution.py:189
  60.6 0.0 copy-start.1
  60.6 0.0 copy-start.2
  60.6 0.0 copy-start.4
  60.6 0.0 copy-start.6
  60.7 0.0 reduce-scatter.2.cloned.1.call-update
  60.7 2.4 %collective-permute-start.1 = (bf16[1,1,128,4096]{3,2,1,0:T(8,128)(2,1)}, bf16[1,1,128,4096]{3,2,1,0:T(8,128)(2,1)S(1)}, u32[]{:S(2)}, u32[]{:S(2)}) collective-permute-start(bf16[1,1,128,4096]{3,2,1,0:T(8,128)(2,1)} %param.10), channel_id=1, source_target_pairs={{0,8},{8,16},{16,24},{24,0},{1,9},{9,17},{17,25},{25,1},{2,10},{10... | collective-permute-start | bytes 3145736 | tf_op jit(solution)/shard_map/ppermute | solution.py:25
  63.7 14.6 %all-gather = f32[8,1,4096]{2,1,0:T(1,128)S(1)} all-gather(f32[1,1,4096]{2,1,0:T(1,128)S(1)} %bitcast.17), channel_id=1, replica_groups=mesh['section'=4,'fork'=8] {'fork'}, dimensions={0}, use_global_device_ids=true | all-gather | bytes 147456 | tf_op jit(solution)/shard_map/all_gather | solution.py:240
  78.3 0.7 reduce_sum.9
  79.1 7.9 %collective-permute-done.1 = bf16[1,1,128,4096]{3,2,1,0:T(8,128)(2,1)S(1)} collective-permute-done((bf16[1,1,128,4096]{3,2,1,0:T(8,128)(2,1)}, bf16[1,1,128,4096]{3,2,1,0:T(8,128)(2,1)S(1)}, u32[]{:S(2)}, u32[]{:S(2)}) %collective-permute-start.1) | collective-permute-done | bytes 1048608 | tf_op jit(solution)/shard_map/ppermute | solution.py:25
  87.0 0.0 copy-done.1
  87.0 0.0 copy-done.2
  87.0 0.0 copy-done.4
  87.0 0.0 copy-done.6
  87.0 6.8 %forward.1 = bf16[128,4096]{1,0:T(8,128)(2,1)} custom-call(s32[16]{0:T(128)S(1)} %bitcast.19, s32[1]{0:T(128)S(6)} %copy.15.length, bf16[128,4096]{1,0:T(8,128)(2,1)S(1)} %bitcast.15, f32[1,4096]{1,0:T(1,128)S(1)} %copy-done.4, bf16[2,512,512]{2,1,0:T(8,128)(2,1)S(1)} %bitcast.14, bf16[2,128,512]{2,1,0:T(8,128)(2,1)S(1)} %bitcast.16), custom_call_target="tpu_custom_call" | custom-call | flops 805306368 | bytes 2097152 | tf_op jit(solution)/shard_map/forward/pallas_call | solution.py:165
  93.8 4.8 %reduce-scatter.2.cloned.1.call-done = f32[1,2,64,512]{3,2,1,0:T(8,128)} async-done(((f32[1,2,512,512]{3,2,1,0:T(8,128)}), f32[1,2,64,512]{3,2,1,0:T(8,128)}) %reduce-scatter.2.cloned.1.call-update) | async-done | bytes 262160 | tf_op jit(solution)/shard_map/reduce_scatter | solution.py:239
Async XLA Ops:
  7.2 27.5 %all-gather.3.cloned.1.call-start = ((), (), s32[]{:S(2)}) async-start(), calls=%async_computation.1 | async-start | bytes 1179648 | tf_op jit(solution)/shard_map/all_gather | solution.py:233
  7.9 90.7 %reduce-scatter.2.cloned.1.call-start = ((), (), s32[]{:S(2)}) async-start(), calls=%async_computation.2 | async-start | bytes 2359296 | tf_op jit(solution)/shard_map/reduce_scatter | solution.py:239
  7.9 26.7 %collective-permute-start = (bf16[1,1,128,4096]{3,2,1,0:T(8,128)(2,1)}, bf16[1,1,128,4096]{3,2,1,0:T(8,128)(2,1)S(1)}, u32[]{:S(2)}, u32[]{:S(2)}) collective-permute-start(bf16[1,1,128,4096]{3,2,1,0:T(8,128)(2,1)} %param.12), channel_id=1, source_target_pairs={{0,24},{8,0},{16,8},{24,16},{1,25},{9,1},{17,9},{25,17},{2,26},{10... | collective-permute-start | bytes 3145736 | tf_op jit(solution)/shard_map/ppermute | solution.py:25
  34.6 1.2 %copy-start = (bf16[1,2,512,512]{3,2,1,0:T(8,128)(2,1)S(1)}, bf16[1,2,512,512]{3,2,1,0:T(8,128)(2,1)}, u32[]{:S(2)}) copy-start(bf16[1,2,512,512]{3,2,1,0:T(8,128)(2,1)} %all-gather.3.cloned.1.call-done) | copy-start | bytes 3145732
  35.9 0.7 copy-start.3
  36.6 0.7 copy-start.5
  37.2 1.2 %copy-start.7 = (bf16[1,1,128,4096]{3,2,1,0:T(8,128)(2,1)S(1)}, bf16[1,1,128,4096]{3,2,1,0:T(8,128)(2,1)}, u32[]{:S(2)}) copy-start(bf16[1,1,128,4096]{3,2,1,0:T(8,128)(2,1)} %param.11) | copy-start | bytes 3145732
  38.5 0.9 copy-start.8
  60.6 26.3 %copy-start.1 = (bf16[1,2,512,512]{3,2,1,0:T(8,128)(2,1)S(1)}, bf16[1,2,512,512]{3,2,1,0:T(8,128)(2,1)}, u32[]{:S(2)}) copy-start(bf16[1,2,512,512]{3,2,1,0:T(8,128)(2,1)} %all-gather.3.cloned.1.call-done) | copy-start | bytes 3145732
  60.6 26.3 %copy-start.2 = (bf16[1,1,2,128,512]{4,3,2,1,0:T(8,128)(2,1)S(1)}, bf16[1,1,2,128,512]{4,3,2,1,0:T(8,128)(2,1)}, u32[]{:S(2)}) copy-start(bf16[1,1,2,128,512]{4,3,2,1,0:T(8,128)(2,1)} %param.14) | copy-start | bytes 786436
  60.6 26.3 %copy-start.4 = (f32[1,4096]{1,0:T(1,128)S(1)}, f32[1,4096]{1,0:T(1,128)}, u32[]{:S(2)}) copy-start(f32[1,4096]{1,0:T(1,128)} %gain.3) | copy-start | bytes 49156
  60.6 26.3 %copy-start.6 = (s32[1,16]{1,0:T(1,128)S(1)}, s32[1,16]{1,0:T(1,128)}, u32[]{:S(2)}) copy-start(s32[1,16]{1,0:T(1,128)} %param.17) | copy-start | bytes 196
  60.7 26.3 %collective-permute-start.1 = (bf16[1,1,128,4096]{3,2,1,0:T(8,128)(2,1)}, bf16[1,1,128,4096]{3,2,1,0:T(8,128)(2,1)S(1)}, u32[]{:S(2)}, u32[]{:S(2)}) collective-permute-start(bf16[1,1,128,4096]{3,2,1,0:T(8,128)(2,1)} %param.10), channel_id=1, source_target_pairs={{0,8},{8,16},{16,24},{24,0},{1,9},{9,17},{17,25},{25,1},{2,10},{10... | collective-permute-start | bytes 3145736 | tf_op jit(solution)/shard_map/ppermute | solution.py:25
Sparse Core Ops, SparseCore 0:
  9.6 24.7 all-gather.2
  60.8 37.7 reduce-scatter.1

commit v2 on v1

--- a/solution.py
+++ b/solution.py
@@ -1,3 +1,4 @@
+import functools
 import math
 
 import jax
@@ -16,7 +17,7 @@
 masked_score = -1e30
 scale = HD ** (-0.5)
 exp_scale = scale * math.log2(math.e)
-vmem_limit = 48 * 1024 * 1024
+vmem_limit = 52 * 1024 * 1024
 
 
 def shifted_2(value, axis, steps):
@@ -93,68 +94,298 @@
             out[:, place] = (x[:, place].astype(jnp.float32) + valid * attended).astype(out.dtype)
 
 
+def chances_kernel(table, length, x, gain, pool, own, chances, queries, inverses, keys, values):
+    rows, width = x.shape
+    group = width // KV
+    g = pl.program_id(0)
+
+    @pl.when(g == 0)
+    def _():
+        gather_rows(table, pool, own, keys, 0)
+        gather_rows(table, pool, own, values, 1)
+        norm_rows(x, gain, queries, inverses)
+
+    mask = key_mask(rows, length[0])
+    k_group = keys[:, pl.ds(pl.multiple_of(g * HD, HD), HD)]
+    for h in range(group // HD):
+        place = pl.ds(pl.multiple_of(g * group + h * HD, HD), HD)
+        chances[0, :, h * HD : (h + 1) * HD] = chances_of(queries[:, place], k_group, mask)
+
+
 def backward_kernel(
-    table, length, x, gain, pool, own, cotangent,
+    table, length, x, gain, cotangent, chances, queries, inverses, keys, values,
     input_grad, pool_grad, own_grad, gain_grad,
-    queries, inverses, keys, values, outs, weights, d_scores, d_queries, d_key, d_value,
+    outs, weights, d_scores, d_queries, d_key, d_value,
 ):
     rows, width = x.shape
     group = width // KV
+    heads = group // HD
     prompt_count = table.shape[0] * BLOCK
-    pool_grad[...] = jnp.zeros_like(pool_grad)
-    gather_rows(table, pool, own, keys, 0)
-    gather_rows(table, pool, own, values, 1)
-    norm_rows(x, gain, queries, inverses)
-    mask = key_mask(rows, length[0])
+    g = pl.program_id(0)
+
+    @pl.when(g == 0)
+    def _():
+        pool_grad[...] = jnp.zeros_like(pool_grad)
+        gain_grad[...] = jnp.zeros_like(gain_grad)
+
     valid = (lax.broadcasted_iota(jnp.int32, (rows, HD), 0) < length[0]).astype(jnp.float32)
-
-    @pl.loop(0, KV)
-    def _(g):
-        columns = pl.ds(pl.multiple_of(g * HD, HD), HD)
-        k_group = keys[:, columns]
-        v_group = values[:, columns]
-        heads = group // HD
-        for h in range(heads):
-            place = pl.ds(pl.multiple_of(g * group + h * HD, HD), HD)
-            spot = slice(h * HD, (h + 1) * HD)
-            q_head = queries[:, place]
-            out_grad = (valid * cotangent[:, place].astype(jnp.float32)).astype(jnp.bfloat16)
-            outs[spot, :] = out_grad
-            chances = chances_of(q_head, k_group, mask)
-            weights[:, spot] = chances.astype(jnp.bfloat16)
-            d_weight = dot(v_group, out_grad, 1, 1)
-            delta = jnp.sum(chances * d_weight, axis=0, keepdims=True)
-            d_score = (chances * (d_weight - delta) * scale).astype(jnp.bfloat16)
-            d_scores[:, spot] = d_score
-            d_queries[:, place] = dot(k_group, d_score, 0, 0).T
-        q_all = jnp.concatenate(
-            [queries[:, pl.ds(pl.multiple_of(g * group + h * HD, HD), HD)] for h in range(heads)], axis=0
-        )
-        d_value[...] = dot(weights[...], outs[...], 1, 0)
-        d_key[...] = dot(d_scores[...], q_all, 1, 0)
-        own_grad[0, :, columns] = d_key[prompt_count:, :]
-        own_grad[1, :, columns] = d_value[prompt_count:, :]
-
-        @pl.loop(0, table.shape[0])
-        def _(j):
-            target = pl.ds(pl.multiple_of(table[j] * BLOCK, BLOCK), BLOCK)
-            source = pl.ds(pl.multiple_of(j * BLOCK, BLOCK), BLOCK)
-            pool_grad[0, target, columns] = d_key[source, :]
-            pool_grad[1, target, columns] = d_value[source, :]
-
-    gain_grad[...] = jnp.zeros_like(gain_grad)
-
-    @pl.loop(0, rows // BLOCK)
-    def _(i):
-        place = pl.ds(pl.multiple_of(i * BLOCK, BLOCK), BLOCK)
-        floated = x[place, :].astype(jnp.float32)
-        inverse = inverses[place, 0:1]
-        d_query = d_queries[place, :]
-        d_normed = d_query * gain[...]
-        along = jnp.mean(d_normed * floated, axis=-1, keepdims=True)
-        d_input = inverse * d_normed - floated * (inverse * inverse * inverse * along)
-        input_grad[place, :] = (cotangent[place, :].astype(jnp.float32) + d_input).astype(input_grad.dtype)
-        gain_grad[...] += jnp.sum(d_query * floated * inverse, axis=0, keepdims=True)
+    columns = pl.ds(pl.multiple_of(g * HD, HD), HD)
+    k_group = keys[:, columns]
+    v_group = values[:, columns]
+    for h in range(heads):
+        place = pl.ds(pl.multiple_of(g * group + h * HD, HD), HD)
+        spot = slice(h * HD, (h + 1) * HD)
+        out_grad = (valid * cotangent[:, place].astype(jnp.float32)).astype(jnp.bfloat16)
+        outs[spot, :] = out_grad
+        chance = chances[0, :, spot]
+        weights[:, spot] = chance.astype(jnp.bfloat16)
+        d_weight = dot(v_group, out_grad, 1, 1)
+        delta = jnp.sum(chance * d_weight, axis=0, keepdims=True)
+        d_score = (chance * (d_weight - delta) * scale).astype(jnp.bfloat16)
+        d_scores[:, spot] = d_score
+        d_queries[:, place] = dot(k_group, d_score, 0, 0).T
+    q_all = jnp.concatenate(
+        [queries[:, pl.ds(pl.multiple_of(g * group + h * HD, HD), HD)] for h in range(heads)], axis=0
+    )
+    d_value[...] = dot(weights[...], outs[...], 1, 0)
+    d_key[...] = dot(d_scores[...], q_all, 1, 0)
+    own_grad[0, :, columns] = d_key[prompt_count:, :]
+    own_grad[1, :, columns] = d_value[prompt_count:, :]
+
+    @pl.loop(0, table.shape[0])
+    def _(j):
+        target = pl.ds(pl.multiple_of(table[j] * BLOCK, BLOCK), BLOCK)
+        source = pl.ds(pl.multiple_of(j * BLOCK, BLOCK), BLOCK)
+        pool_grad[0, target, columns] = d_key[source, :]
+        pool_grad[1, target, columns] = d_value[source, :]
+
+    @pl.when(g == KV - 1)
+    def _():
+        @pl.loop(0, rows // BLOCK)
+        def _(i):
+            place = pl.ds(pl.multiple_of(i * BLOCK, BLOCK), BLOCK)
+            floated = x[place, :].astype(jnp.float32)
+            inverse = inverses[place, 0:1]
+            d_query = d_queries[place, :]
+            d_normed = d_query * gain[...]
+            along = jnp.mean(d_normed * floated, axis=-1, keepdims=True)
+            d_input = inverse * d_normed - floated * (inverse * inverse * inverse * along)
+            input_grad[place, :] = (cotangent[place, :].astype(jnp.float32) + d_input).astype(input_grad.dtype)
+            gain_grad[...] += jnp.sum(d_query * floated * inverse, axis=0, keepdims=True)
+
+
+def share_kernel(
+    devices, part, gain_part, prompt_grad, gain_grad,
+    paired, outgoing, arrived, gain_paired, gains,
+    send_a, recv_a, send_b, recv_b, send_g, recv_g, send_p, recv_p,
+):
+    chips = devices // 2
+    rows = prompt_grad.shape[1]
+    me = lax.axis_index("fork")
+    chip, core = me // 2, lax.rem(me, 2)
+    twin = chip * 2 + (1 - core)
+    mesh_type = pl.DeviceIdType.MESH
+
+    def slot(c, parity):
+        return pl.ds(pl.multiple_of((c * 2 + parity) * rows, rows), rows)
+
+    def after(d):
+        return lax.rem(chip + d, chips)
+
+    def pair_copy(c):
+        return pltpu.make_async_remote_copy(
+            src_ref=part.at[:, slot(c, 1 - core), :], dst_ref=paired.at[c],
+            send_sem=send_a.at[c], recv_sem=recv_a.at[c],
+            device_id={"fork": twin}, device_id_type=mesh_type,
+        )
+
+    def chip_copy(to, origin):
+        return pltpu.make_async_remote_copy(
+            src_ref=outgoing.at[to], dst_ref=arrived.at[origin],
+            send_sem=send_b.at[to], recv_sem=recv_b.at[origin],
+            device_id={"fork": to * 2 + core}, device_id_type=mesh_type,
+        )
+
+    def gain_copy(to, origin):
+        return pltpu.make_async_remote_copy(
+            src_ref=gains.at[chip], dst_ref=gains.at[origin],
+            send_sem=send_g.at[to], recv_sem=recv_g.at[origin],
+            device_id={"fork": to * 2 + core}, device_id_type=mesh_type,
+        )
+
+    gain_pair = pltpu.make_async_remote_copy(
+        src_ref=gain_part, dst_ref=gain_paired, send_sem=send_p, recv_sem=recv_p,
+        device_id={"fork": twin}, device_id_type=mesh_type,
+    )
+
+    barrier = pltpu.get_barrier_semaphore()
+    pl.semaphore_signal(barrier, inc=1, device_id={"fork": twin}, device_id_type=mesh_type)
+
+    @pl.loop(1, chips)
+    def _(d):
+        pl.semaphore_signal(
+            barrier, inc=1, device_id={"fork": after(d) * 2 + core}, device_id_type=mesh_type
+        )
+
+    pl.semaphore_wait(barrier, chips)
+
+    gain_pair.start()
+
+    @pl.loop(1, chips + 1)
+    def _(d):
+        pair_copy(after(d)).start()
+
+    gain_pair.wait()
+    gains[chip] = gain_part[...] + gain_paired[...]
+
+    @pl.loop(1, chips)
+    def _(d):
+        gain_copy(after(d), chip).start()
+
+    @pl.loop(1, chips)
+    def _(d):
+        to = after(d)
+        pair_copy(to).wait()
+        outgoing[to] = (part[:, slot(to, core), :] + paired[to]).astype(outgoing.dtype)
+        chip_copy(to, chip).start()
+
+    pair_copy(chip).wait()
+    prompt_grad[...] = part[:, slot(chip, core), :] + paired[chip]
+
+    @pl.loop(1, chips)
+    def _(d):
+        origin = lax.rem(chip + chips - d, chips)
+        gain_copy(after(d), chip).wait_send()
+        gain_copy(after(d), origin).wait_recv()
+
+    total = gains[0]
+    for c in range(1, chips):
+        total = total + gains[c]
+    gain_grad[...] = total
+
+    @pl.loop(1, chips)
+    def _(d):
+        origin = lax.rem(chip + chips - d, chips)
+        chip_copy(after(d), origin).wait_recv()
+        prompt_grad[...] += arrived[origin].astype(jnp.float32)
+
+    @pl.loop(1, chips)
+    def _(d):
+        chip_copy(after(d), chip).wait_send()
+
+
+def collect_kernel(devices, part, pool, send_a, recv_a, send_b, recv_b):
+    chips = devices // 2
+    rows = part.shape[1]
+    me = lax.axis_index("fork")
+    chip, core = me // 2, lax.rem(me, 2)
+    twin = chip * 2 + (1 - core)
+    mesh_type = pl.DeviceIdType.MESH
+
+    def slot(c, parity):
+        return pl.ds(pl.multiple_of((c * 2 + parity) * rows, rows), rows)
+
+    def after(d):
+        return lax.rem(chip + d, chips)
+
+    def twin_copy(c, parity):
+        return pltpu.make_async_remote_copy(
+            src_ref=pool.at[:, slot(c, parity), :], dst_ref=pool.at[:, slot(c, parity), :],
+            send_sem=send_a.at[c], recv_sem=recv_a.at[c],
+            device_id={"fork": twin}, device_id_type=mesh_type,
+        )
+
+    def chip_copy(to, origin):
+        return pltpu.make_async_remote_copy(
+            src_ref=part, dst_ref=pool.at[:, slot(origin, core), :],
+            send_sem=send_b.at[to], recv_sem=recv_b.at[origin],
+            device_id={"fork": to * 2 + core}, device_id_type=mesh_type,
+        )
+
+    barrier = pltpu.get_barrier_semaphore()
+    pl.semaphore_signal(barrier, inc=1, device_id={"fork": twin}, device_id_type=mesh_type)
+
+    @pl.loop(1, chips)
+    def _(d):
+        pl.semaphore_signal(
+            barrier, inc=1, device_id={"fork": after(d) * 2 + core}, device_id_type=mesh_type
+        )
+
+    pl.semaphore_wait(barrier, chips)
+
+    @pl.loop(1, chips)
+    def _(d):
+        chip_copy(after(d), chip).start()
+
+    pool[:, slot(chip, core), :] = part[...]
+    twin_copy(chip, core).start()
+
+    @pl.loop(1, chips)
+    def _(d):
+        origin = lax.rem(chip + chips - d, chips)
+        chip_copy(after(d), origin).wait_recv()
+        twin_copy(origin, core).start()
+
+    @pl.loop(0, chips)
+    def _(c):
+        twin_copy(c, core).wait_send()
+        twin_copy(c, 1 - core).wait_recv()
+
+    @pl.loop(1, chips)
+    def _(d):
+        chip_copy(after(d), chip).wait_send()
+
+
+def collect(part):
+    devices = lax.axis_size("fork")
+    chips = devices // 2
+    kinds, rows, width = part.shape
+    vmem = pl.BlockSpec(memory_space=pltpu.VMEM)
+    several = pltpu.SemaphoreType.DMA((chips,))
+    return pl.pallas_call(
+        functools.partial(collect_kernel, devices),
+        out_shape=jax.ShapeDtypeStruct((kinds, rows * devices, width), part.dtype),
+        in_specs=[vmem],
+        out_specs=vmem,
+        scratch_shapes=[several, several, several, several],
+        compiler_params=pltpu.CompilerParams(
+            collective_id=1, has_side_effects=True, vmem_limit_bytes=vmem_limit
+        ),
+        cost_estimate=pl.CostEstimate(flops=part.size, bytes_accessed=part.size * 16, transcendentals=0),
+        name="collect",
+    )(part)
+
+
+def share(part, gain_part):
+    devices = lax.axis_size("fork")
+    chips = devices // 2
+    kinds, total, width = part.shape
+    rows = total // devices
+    vmem = pl.BlockSpec(memory_space=pltpu.VMEM)
+    several = pltpu.SemaphoreType.DMA((chips,))
+    single = pltpu.SemaphoreType.DMA
+    return pl.pallas_call(
+        functools.partial(share_kernel, devices),
+        out_shape=(
+            jax.ShapeDtypeStruct((kinds, rows, width), jnp.float32),
+            jax.ShapeDtypeStruct(gain_part.shape, jnp.float32),
+        ),
+        in_specs=[vmem, vmem],
+        out_specs=(vmem, vmem),
+        scratch_shapes=[
+            pltpu.VMEM((chips, kinds, rows, width), jnp.float32),
+            pltpu.VMEM((chips, kinds, rows, width), jnp.bfloat16),
+            pltpu.VMEM((chips, kinds, rows, width), jnp.bfloat16),
+            pltpu.VMEM(gain_part.shape, jnp.float32),
+            pltpu.VMEM((chips,) + gain_part.shape, jnp.float32),
+            several, several, several, several, several, several, single, single,
+        ],
+        compiler_params=pltpu.CompilerParams(
+            collective_id=0, has_side_effects=True, vmem_limit_bytes=vmem_limit
+        ),
+        cost_estimate=pl.CostEstimate(flops=part.size, bytes_accessed=part.size * 4, transcendentals=0),
+        name="share",
+    )(part, gain_part)
 
 
 def forward(table, length, x, gain, pool, own):
@@ -180,27 +411,62 @@
     )(table, length, x, gain, pool, own)
 
 
-def backward(table, length, x, gain, pool, own, cotangent):
+def whole_block(shape):
+    return pl.BlockSpec(shape, lambda g: (0,) * len(shape))
+
+
+def chances_call(table, length, x, gain, pool, own):
     rows, width = x.shape
     count = table.shape[0] * BLOCK + rows
     group = width // KV
-    vmem = pl.BlockSpec(memory_space=pltpu.VMEM)
     smem = pl.BlockSpec(memory_space=pltpu.SMEM)
     return pl.pallas_call(
+        chances_kernel,
+        grid=(KV,),
+        out_shape=(
+            jax.ShapeDtypeStruct((KV, count, group), jnp.float32),
+            jax.ShapeDtypeStruct(x.shape, jnp.bfloat16),
+            jax.ShapeDtypeStruct((rows, HD), jnp.float32),
+            jax.ShapeDtypeStruct((count, pool.shape[-1]), jnp.bfloat16),
+            jax.ShapeDtypeStruct((count, pool.shape[-1]), jnp.bfloat16),
+        ),
+        in_specs=[smem, smem] + [whole_block(v.shape) for v in (x, gain, pool, own)],
+        out_specs=(
+            pl.BlockSpec((1, count, group), lambda g: (g, 0, 0)),
+            whole_block(x.shape),
+            whole_block((rows, HD)),
+            whole_block((count, pool.shape[-1])),
+            whole_block((count, pool.shape[-1])),
+        ),
+        compiler_params=pltpu.CompilerParams(vmem_limit_bytes=vmem_limit),
+        cost_estimate=pl.CostEstimate(
+            flops=2 * rows * width * count, bytes_accessed=10 * rows * width, transcendentals=rows * width // HD * count
+        ),
+        name="chances",
+    )(table, length, x, gain, pool, own)
+
+
+def backward(table, length, x, gain, pool, own, cotangent, held):
+    rows, width = x.shape
+    count = table.shape[0] * BLOCK + rows
+    group = width // KV
+    smem = pl.BlockSpec(memory_space=pltpu.SMEM)
+    outs = (
+        jax.ShapeDtypeStruct(x.shape, x.dtype),
+        jax.ShapeDtypeStruct(pool.shape, jnp.float32),
+        jax.ShapeDtypeStruct(own.shape, jnp.float32),
+        jax.ShapeDtypeStruct((1, width), jnp.float32),
+    )
+    return pl.pallas_call(
         backward_kernel,
-        out_shape=(
-            jax.ShapeDtypeStruct(x.shape, x.dtype),
-            jax.ShapeDtypeStruct(pool.shape, jnp.float32),
-            jax.ShapeDtypeStruct(own.shape, jnp.float32),
-            jax.ShapeDtypeStruct((1, width), jnp.float32),
-        ),
-        in_specs=[smem, smem] + [vmem] * 5,
-        out_specs=(vmem,) * 4,
+        grid=(KV,),
+        out_shape=outs,
+        in_specs=[smem, smem]
+        + [whole_block(v.shape) for v in (x, gain, cotangent)]
+        + [pl.BlockSpec((1, count, group), lambda g: (g, 0, 0))]
+        + [whole_block(v.shape) for v in held[1:]],
+        out_specs=tuple(whole_block(v.shape) for v in outs),
         scratch_shapes=[
-            pltpu.VMEM((rows, width), jnp.bfloat16),
-            pltpu.VMEM((rows, HD), jnp.float32),
-            pltpu.VMEM((count, pool.shape[-1]), jnp.bfloat16),
-            pltpu.VMEM((count, pool.shape[-1]), jnp.bfloat16),
             pltpu.VMEM((rows * group // HD, HD), jnp.bfloat16),
             pltpu.VMEM((count, group), jnp.bfloat16),
             pltpu.VMEM((count, group), jnp.bfloat16),
@@ -210,10 +476,10 @@
         ],
         compiler_params=pltpu.CompilerParams(vmem_limit_bytes=vmem_limit),
         cost_estimate=pl.CostEstimate(
-            flops=10 * rows * width * count, bytes_accessed=10 * rows * width, transcendentals=rows * width // HD * count
+            flops=80 * rows * width * count, bytes_accessed=20 * rows * width, transcendentals=0
         ),
         name="backward",
-    )(table, length, x, gain, pool, own, cotangent)
+    )(table, length, x, gain, cotangent, *held)
 
 
 def shards(
@@ -230,23 +496,24 @@
 ):
     cotangent = shifted_2(returning, "section", -1)
     table = block_tables[0]
-    pool = lax.all_gather(prompt_cache, "fork", axis=2, tiled=True)[0]
-    arriving, cotangent = lax.optimization_barrier((arriving, cotangent))
+    pool = collect(prompt_cache[0])
+    held = chances_call(table, back_lengths, saved_input[0, 0], query_gain, pool, back_cache[0, 0])
+    arriving, cotangent, inverses = lax.optimization_barrier((arriving, cotangent, held[2]))
+    held = held[:2] + (inverses,) + held[3:]
     incoming = shifted_2(arriving, "section", 1)
     input_grad, pool_grad, own_grad, gain_part = backward(
-        table, back_lengths, saved_input[0, 0], query_gain, pool, back_cache[0, 0], cotangent[0, 0]
-    )
-    prompt_grad = lax.psum_scatter(pool_grad[None], "fork", scatter_dimension=2, tiled=True)
-    gain_parts = lax.all_gather(gain_part, "fork", axis=0, tiled=True)
+        table, back_lengths, saved_input[0, 0], query_gain, pool, back_cache[0, 0], cotangent[0, 0], held
+    )
+    prompt_grad, gain_grad = share(pool_grad, gain_part)
     section_output = forward(
         table, fresh_lengths, incoming[0, 0], query_gain, pool, fresh_cache[0, 0]
     )
     return (
         section_output[None, None],
         input_grad[None, None],
-        prompt_grad,
+        prompt_grad[None],
         own_grad[None, None],
-        jnp.sum(gain_parts, axis=0, keepdims=True),
+        gain_grad,
     )
 
 

time: 106 us -> 76.4 us (0.72)
  waiting for transfers between devices: 35.5 us -> 0.01 us
  Pallas kernels: 28.1 us -> 61.7 us
  blocking collectives: 14.6 us -> 0 us
  between operations: 15.4 us -> 2 us
  local copies, waits for them, and re-layouts: 4.79 us -> 7.73 us
  starting transfers between devices: 6.4 us -> 4 us
    pallas_call x1 -> x4, Pallas kernels: 21.2 us -> 54.2 us  [the longest x1 18.5 us: share(): pl.pallas_call(functools.partial(share_kernel, devices), out_shape=(jax.S...]
    ppermute x2, waiting for transfers between devices: 30 us -> 0.01 us  [shifted_2(): return lax.ppermute(value, axis, pairs)]
    all_gather x1 -> x0, blocking collectives: 14.6 us -> none  [shards(): gain_parts = lax.all_gather(gain_part, 'fork', axis=0, tiled=True)]
    reduce_scatter x1 -> x0, waiting for transfers between devices: 4.82 us -> none  [shards(): lax.psum_scatter(pool_grad[None], 'fork', scatter_dimension=2, tiled=True)]
    unnamed x18 -> x20, local copies, waits for them, and re-layouts: 4.79 us -> 7.73 us
    ppermute x2, starting transfers between devices: 6.32 us -> 4 us  [shifted_2(): return lax.ppermute(value, axis, pairs)]
  transfers between devices with their start and end apart: 4 -> 2, of which waited for: 3 -> 0; matrix products, arithmetic and copies ran while one was open for 1% -> 0% of each run, Pallas kernels for 6% -> 72%
where the time goes in v2:
time: 76.4 us; the launch traced here: 75.4 us
  Pallas kernels  61.7 us (81%)
  local copies, waits for them, and re-layouts  7.73 us (10%)
  starting transfers between devices  4 us (5%)
  between operations  2 us (3%)
    pallas_call x1, Pallas kernels, share(): pl.pallas_call(functools.partial(share_kernel, devices), out_shape=(jax.S...  18.5 us
    pallas_call x1, Pallas kernels, collect(): pl.pallas_call(functools.partial(collect_kernel, devices), out_shape=jax....  14.9 us
    pallas_call x1, Pallas kernels, backward(): pl.pallas_call(backward_kernel, grid=(KV,), out_shape=outs, in_specs=[sme...  13.1 us
    unnamed x20, local copies, waits for them, and re-layouts  7.73 us
    pallas_call x1, Pallas kernels, chances_call(): pl.pallas_call(chances_kernel, grid=(KV,), out_shape=(jax.ShapeDtypeStruc...  7.66 us
    pallas_call x1, Pallas kernels, forward(): pl.pallas_call(forward_kernel, out_shape=jax.ShapeDtypeStruct(x.shape, x....  7.52 us
    ppermute x2, starting transfers between devices, shifted_2(): return lax.ppermute(value, axis, pairs)  4 us
  transfers between devices with their start and end apart: 2, of which 0 were waited for; matrix products, arithmetic and copies ran while one was open for 0% of the time, Pallas kernels for 72%

profile of v2, /device:TPU:0, one launch (start us, length us, event | category | flops | bytes accessed | tf_op | source)
XLA Modules:
  0.0 75.4 jit_solution(5994566262576959679)
XLA Ops:
  0.6 3.9 %collective-permute-start = (bf16[1,1,128,4096]{3,2,1,0:T(8,128)(2,1)}, bf16[1,1,128,4096]{3,2,1,0:T(8,128)(2,1)S(1)}, u32[]{:S(2)}, u32[]{:S(2)}) collective-permute-start(bf16[1,1,128,4096]{3,2,1,0:T(8,128)(2,1)} %param.12), channel_id=1, source_target_pairs={{0,24},{8,0},{16,8},{24,16},{1,25},{9,1},{17,9},{25,17},{2,26},{10... | collective-permute-start | bytes 3145736 | tf_op jit(solution)/shard_map/ppermute | solution.py:26
  4.6 0.0 copy-start.2
  4.6 0.9 %copy-done.2 = bf16[1,2,64,512]{3,2,1,0:T(8,128)(2,1)S(1)} copy-done((bf16[1,2,64,512]{3,2,1,0:T(8,128)(2,1)S(1)}, bf16[1,2,64,512]{3,2,1,0:T(8,128)(2,1)}, u32[]{:S(2)}) %copy-start.2) | copy-done | bytes 131096
  5.5 14.9 %collect.1.pool = bf16[2,512,512]{2,1,0:T(8,128)(2,1)S(1)} custom-call(bf16[2,64,512]{2,1,0:T(8,128)(2,1)S(1)} %bitcast.14), custom_call_target="tpu_custom_call" | custom-call | flops 65536 | bytes 1048576 | tf_op jit(solution)/shard_map/collect/pallas_call | solution.py:345
  20.4 0.0 copy-start
  20.4 1.1 %copy-done = bf16[2,512,512]{2,1,0:T(8,128)(2,1)} copy-done((bf16[2,512,512]{2,1,0:T(8,128)(2,1)}, bf16[2,512,512]{2,1,0:T(8,128)(2,1)S(1)}, u32[]{:S(2)}) %copy-start) | copy-done | bytes 1048600
  22.8 0.0 copy-start.3
  22.8 0.7 copy-done.3
  23.5 0.0 copy-start.5
  23.5 0.7 copy-done.5
  24.1 0.0 copy-start.7
  24.1 0.9 %copy-done.7 = bf16[1,1,2,128,512]{4,3,2,1,0:T(8,128)(2,1)S(1)} copy-done((bf16[1,1,2,128,512]{4,3,2,1,0:T(8,128)(2,1)S(1)}, bf16[1,1,2,128,512]{4,3,2,1,0:T(8,128)(2,1)}, u32[]{:S(2)}) %copy-start.7) | copy-done | bytes 262168
  25.1 7.7 %chances.1 = (f32[4,384,1024]{2,1,0:T(8,128)}, bf16[128,4096]{1,0:T(8,128)(2,1)}, f32[128,128]{1,0:T(8,128)S(1)}, bf16[384,512]{1,0:T(8,128)(2,1)S(1)}, bf16[384,512]{1,0:T(8,128)(2,1)S(1)}) custom-call(s32[16]{0:T(128)S(1)} %bitcast.15, s32[1]{0:T(128)S(6)} %copy.18.length, bf16[128,4096]{1,0:T(8,128)(2,1)} %bitcast.18, f32[1,4096]{1,0:T(1,128)S(1)} %copy-done.3, ...), custom_call_target="tpu_custom_call" | custom-call | flops 402653184 | bytes 5242880 | tf_op jit(solution)/shard_map/chances/pallas_call | solution.py:423
  32.8 0.0 collective-permute-done
  32.8 0.0 copy-start.8
  32.8 0.1 collective-permute-start.1
  32.8 0.9 %copy-done.8 = bf16[1,1,128,4096]{3,2,1,0:T(8,128)(2,1)} copy-done((bf16[1,1,128,4096]{3,2,1,0:T(8,128)(2,1)}, bf16[1,1,128,4096]{3,2,1,0:T(8,128)(2,1)S(1)}, u32[]{:S(2)}) %copy-start.8) | copy-done | bytes 1048600
  33.7 0.0 copy-start.6
  33.7 1.2 %copy-done.6 = bf16[1,1,128,4096]{3,2,1,0:T(8,128)(2,1)S(1)} copy-done((bf16[1,1,128,4096]{3,2,1,0:T(8,128)(2,1)S(1)}, bf16[1,1,128,4096]{3,2,1,0:T(8,128)(2,1)}, u32[]{:S(2)}) %copy-start.6) | copy-done | bytes 1048600
  35.0 0.0 copy-start.1
  35.0 0.0 copy-start.4
  35.0 13.1 %backward.1 = (bf16[128,4096]{1,0:T(8,128)(2,1)}, f32[2,512,512]{2,1,0:T(8,128)}, f32[2,128,512]{2,1,0:T(8,128)}, f32[1,4096]{1,0:T(1,128)S(1)}) custom-call(s32[16]{0:T(128)S(1)} %bitcast.16, s32[1]{0:T(128)S(6)} %copy.18.length, bf16[128,4096]{1,0:T(8,128)(2,1)S(1)} %bitcast.19, f32[1,4096]{1,0:T(1,128)S(1)} %copy-done.3, bf16[128,4096]{1,0:T(8,128)(2,1)} %bitcast.22, ...), custom_call_target="tpu_custom_call" | custom-call | flops 16106127360 | bytes 10485760 | tf_op jit(solution)/shard_map/backward/pallas_call | solution.py:460
  48.0 18.5 %share.1 = (f32[2,64,512]{2,1,0:T(8,128)S(1)}, f32[1,4096]{1,0:T(1,128)S(1)}) custom-call(f32[2,512,512]{2,1,0:T(8,128)} %get-tuple-element.28.part, f32[1,4096]{1,0:T(1,128)S(1)} %get-tuple-element.29.gain_part), custom_call_target="tpu_custom_call" | custom-call | flops 524288 | bytes 2097152 | tf_op jit(solution)/shard_map/share/pallas_call | solution.py:367
  66.6 0.0 collective-permute-done.1
  66.6 0.0 copy-done.1
  66.6 0.0 copy-done.4
  66.6 7.5 %forward.1 = bf16[128,4096]{1,0:T(8,128)(2,1)} custom-call(s32[16]{0:T(128)S(1)} %bitcast.17, s32[1]{0:T(128)S(6)} %copy.17.length, bf16[128,4096]{1,0:T(8,128)(2,1)S(1)} %bitcast.11, f32[1,4096]{1,0:T(1,128)S(1)} %copy-done.4, bf16[2,512,512]{2,1,0:T(8,128)(2,1)} %copy-done, bf16[2,128,512]{2,1,0:T(8,128)(2,1)S(1)} %bitcast.12), custom_call_target="tpu_custom_call" | custom-call | flops 805306368 | bytes 2097152 | tf_op jit(solution)/shard_map/forward/pallas_call | solution.py:396
  74.1 0.7 copy.19
  74.8 0.6 copy.20
Async XLA Ops:
  0.6 32.1 %collective-permute-start = (bf16[1,1,128,4096]{3,2,1,0:T(8,128)(2,1)}, bf16[1,1,128,4096]{3,2,1,0:T(8,128)(2,1)S(1)}, u32[]{:S(2)}, u32[]{:S(2)}) collective-permute-start(bf16[1,1,128,4096]{3,2,1,0:T(8,128)(2,1)} %param.12), channel_id=1, source_target_pairs={{0,24},{8,0},{16,8},{24,16},{1,25},{9,1},{17,9},{25,17},{2,26},{10... | collective-permute-start | bytes 3145736 | tf_op jit(solution)/shard_map/ppermute | solution.py:26
  4.6 0.9 %copy-start.2 = (bf16[1,2,64,512]{3,2,1,0:T(8,128)(2,1)S(1)}, bf16[1,2,64,512]{3,2,1,0:T(8,128)(2,1)}, u32[]{:S(2)}) copy-start(bf16[1,2,64,512]{3,2,1,0:T(8,128)(2,1)} %param.13) | copy-start | bytes 393220
  20.4 1.1 %copy-start = (bf16[2,512,512]{2,1,0:T(8,128)(2,1)}, bf16[2,512,512]{2,1,0:T(8,128)(2,1)S(1)}, u32[]{:S(2)}) copy-start(bf16[2,512,512]{2,1,0:T(8,128)(2,1)S(1)} %collect.1.pool) | copy-start | bytes 3145732
  22.8 0.7 copy-start.3
  23.5 0.7 copy-start.5
  24.1 0.9 %copy-start.7 = (bf16[1,1,2,128,512]{4,3,2,1,0:T(8,128)(2,1)S(1)}, bf16[1,1,2,128,512]{4,3,2,1,0:T(8,128)(2,1)}, u32[]{:S(2)}) copy-start(bf16[1,1,2,128,512]{4,3,2,1,0:T(8,128)(2,1)} %param.15) | copy-start | bytes 786436
  32.8 1.0 %copy-start.8 = (bf16[1,1,128,4096]{3,2,1,0:T(8,128)(2,1)}, bf16[1,1,128,4096]{3,2,1,0:T(8,128)(2,1)S(1)}, u32[]{:S(2)}) copy-start(bf16[1,1,128,4096]{3,2,1,0:T(8,128)(2,1)S(1)} %collective-permute-done) | copy-start | bytes 3145732
  32.8 33.8 %collective-permute-start.1 = (bf16[1,1,128,4096]{3,2,1,0:T(8,128)(2,1)}, bf16[1,1,128,4096]{3,2,1,0:T(8,128)(2,1)S(1)}, u32[]{:S(2)}, u32[]{:S(2)}) collective-permute-start(bf16[1,1,128,4096]{3,2,1,0:T(8,128)(2,1)} %param.10), channel_id=1, source_target_pairs={{0,8},{8,16},{16,24},{24,0},{1,9},{9,17},{17,25},{25,1},{2,10},{10... | collective-permute-start | bytes 3145736 | tf_op jit(solution)/shard_map/ppermute | solution.py:26
  33.7 1.2 %copy-start.6 = (bf16[1,1,128,4096]{3,2,1,0:T(8,128)(2,1)S(1)}, bf16[1,1,128,4096]{3,2,1,0:T(8,128)(2,1)}, u32[]{:S(2)}) copy-start(bf16[1,1,128,4096]{3,2,1,0:T(8,128)(2,1)} %param.11) | copy-start | bytes 3145732
  35.0 31.6 %copy-start.1 = (bf16[1,1,2,128,512]{4,3,2,1,0:T(8,128)(2,1)S(1)}, bf16[1,1,2,128,512]{4,3,2,1,0:T(8,128)(2,1)}, u32[]{:S(2)}) copy-start(bf16[1,1,2,128,512]{4,3,2,1,0:T(8,128)(2,1)} %param.14) | copy-start | bytes 786436
  35.0 31.6 %copy-start.4 = (f32[1,4096]{1,0:T(1,128)S(1)}, f32[1,4096]{1,0:T(1,128)}, u32[]{:S(2)}) copy-start(f32[1,4096]{1,0:T(1,128)} %gain.5) | copy-start | bytes 49156

commit v3 on v2

--- a/solution.py
+++ b/solution.py
@@ -11,13 +11,14 @@
 KV = 4
 HD = 128
 BLOCK = 16
+TOGETHER = 2
 
 
 epsilon = 1e-06
 masked_score = -1e30
 scale = HD ** (-0.5)
 exp_scale = scale * math.log2(math.e)
-vmem_limit = 52 * 1024 * 1024
+vmem_limit = 60 * 1024 * 1024
 
 
 def shifted_2(value, axis, steps):
@@ -56,9 +57,17 @@
 
 
 def key_mask(rows, length):
-    key = lax.broadcasted_iota(jnp.int32, (rows, rows), 0)
-    row = lax.broadcasted_iota(jnp.int32, (rows, rows), 1)
+    key = lax.broadcasted_iota(jnp.int32, (rows, TOGETHER * rows), 0)
+    row = lax.rem(lax.broadcasted_iota(jnp.int32, (rows, TOGETHER * rows), 1), rows)
     return (key <= row) & (key < length)
+
+
+def head_place(g, group, h):
+    return pl.ds(pl.multiple_of(g * group + h * HD, HD), HD)
+
+
+def heads_of(ref, g, group, first, count):
+    return jnp.concatenate([ref[:, head_place(g, group, first + k)] for k in range(count)], axis=0)
 
 
 def chances_of(q_head, keys, mask):
@@ -87,11 +96,13 @@
         columns = pl.ds(pl.multiple_of(g * HD, HD), HD)
         k_group = keys[:, columns]
         v_group = values[:, columns]
-        for h in range(group // HD):
-            place = pl.ds(pl.multiple_of(g * group + h * HD, HD), HD)
-            chances = chances_of(queries[:, place], k_group, mask)
+        for h in range(0, group // HD, TOGETHER):
+            chances = chances_of(heads_of(queries, g, group, h, TOGETHER), k_group, mask)
             attended = dot(v_group, chances.astype(jnp.bfloat16), 0, 0).T
-            out[:, place] = (x[:, place].astype(jnp.float32) + valid * attended).astype(out.dtype)
+            for k in range(TOGETHER):
+                place = head_place(g, group, h + k)
+                piece = attended[k * rows : (k + 1) * rows]
+                out[:, place] = (x[:, place].astype(jnp.float32) + valid * piece).astype(out.dtype)
 
 
 def chances_kernel(table, length, x, gain, pool, own, chances, queries, inverses, keys, values):
@@ -107,9 +118,10 @@
 
     mask = key_mask(rows, length[0])
     k_group = keys[:, pl.ds(pl.multiple_of(g * HD, HD), HD)]
-    for h in range(group // HD):
-        place = pl.ds(pl.multiple_of(g * group + h * HD, HD), HD)
-        chances[0, :, h * HD : (h + 1) * HD] = chances_of(queries[:, place], k_group, mask)
+    for h in range(0, group // HD, TOGETHER):
+        chances[0, :, h * rows : (h + TOGETHER) * rows] = chances_of(
+            heads_of(queries, g, group, h, TOGETHER), k_group, mask
+        )
 
 
 def backward_kernel(
@@ -128,14 +140,15 @@
         pool_grad[...] = jnp.zeros_like(pool_grad)
         gain_grad[...] = jnp.zeros_like(gain_grad)
 
-    valid = (lax.broadcasted_iota(jnp.int32, (rows, HD), 0) < length[0]).astype(jnp.float32)
+    row = lax.rem(lax.broadcasted_iota(jnp.int32, (TOGETHER * rows, HD), 0), rows)
+    valid = (row < length[0]).astype(jnp.float32)
     columns = pl.ds(pl.multiple_of(g * HD, HD), HD)
     k_group = keys[:, columns]
     v_group = values[:, columns]
-    for h in range(heads):
-        place = pl.ds(pl.multiple_of(g * group + h * HD, HD), HD)
-        spot = slice(h * HD, (h + 1) * HD)
-        out_grad = (valid * cotangent[:, place].astype(jnp.float32)).astype(jnp.bfloat16)
+    for h in range(0, heads, TOGETHER):
+        spot = slice(h * rows, (h + TOGETHER) * rows)
+        out_grad = heads_of(cotangent, g, group, h, TOGETHER).astype(jnp.float32)
+        out_grad = (valid * out_grad).astype(jnp.bfloat16)
         outs[spot, :] = out_grad
         chance = chances[0, :, spot]
         weights[:, spot] = chance.astype(jnp.bfloat16)
@@ -143,10 +156,10 @@
         delta = jnp.sum(chance * d_weight, axis=0, keepdims=True)
         d_score = (chance * (d_weight - delta) * scale).astype(jnp.bfloat16)
         d_scores[:, spot] = d_score
-        d_queries[:, place] = dot(k_group, d_score, 0, 0).T
-    q_all = jnp.concatenate(
-        [queries[:, pl.ds(pl.multiple_of(g * group + h * HD, HD), HD)] for h in range(heads)], axis=0
-    )
+        d_query = dot(k_group, d_score, 0, 0).T
+        for k in range(TOGETHER):
+            d_queries[:, head_place(g, group, h + k)] = d_query[k * rows : (k + 1) * rows]
+    q_all = heads_of(queries, g, group, 0, heads)
     d_value[...] = dot(weights[...], outs[...], 1, 0)
     d_key[...] = dot(d_scores[...], q_all, 1, 0)
     own_grad[0, :, columns] = d_key[prompt_count:, :]
@@ -424,7 +437,7 @@
         chances_kernel,
         grid=(KV,),
         out_shape=(
-            jax.ShapeDtypeStruct((KV, count, group), jnp.float32),
+            jax.ShapeDtypeStruct((KV, count, group // HD * rows), jnp.float32),
             jax.ShapeDtypeStruct(x.shape, jnp.bfloat16),
             jax.ShapeDtypeStruct((rows, HD), jnp.float32),
             jax.ShapeDtypeStruct((count, pool.shape[-1]), jnp.bfloat16),
@@ -432,7 +445,7 @@
         ),
         in_specs=[smem, smem] + [whole_block(v.shape) for v in (x, gain, pool, own)],
         out_specs=(
-            pl.BlockSpec((1, count, group), lambda g: (g, 0, 0)),
+            pl.BlockSpec((1, count, group // HD * rows), lambda g: (g, 0, 0)),
             whole_block(x.shape),
             whole_block((rows, HD)),
             whole_block((count, pool.shape[-1])),
@@ -463,13 +476,13 @@
         out_shape=outs,
         in_specs=[smem, smem]
         + [whole_block(v.shape) for v in (x, gain, cotangent)]
-        + [pl.BlockSpec((1, count, group), lambda g: (g, 0, 0))]
+        + [pl.BlockSpec((1, count, group // HD * rows), lambda g: (g, 0, 0))]
         + [whole_block(v.shape) for v in held[1:]],
         out_specs=tuple(whole_block(v.shape) for v in outs),
         scratch_shapes=[
             pltpu.VMEM((rows * group // HD, HD), jnp.bfloat16),
-            pltpu.VMEM((count, group), jnp.bfloat16),
-            pltpu.VMEM((count, group), jnp.bfloat16),
+            pltpu.VMEM((count, group // HD * rows), jnp.bfloat16),
+            pltpu.VMEM((count, group // HD * rows), jnp.bfloat16),
             pltpu.VMEM((rows, width), jnp.float32),
             pltpu.VMEM((count, HD), jnp.float32),
             pltpu.VMEM((count, HD), jnp.float32),

time: 76.4 us -> 82.6 us (1.081)
  Pallas kernels: 61.7 us -> 70.9 us
  local copies, waits for them, and re-layouts: 7.73 us -> 4.85 us
    pallas_call x1, Pallas kernels: 7.52 us -> 11.5 us  [forward(): pl.pallas_call(forward_kernel, out_shape=jax.ShapeDtypeStruct(x.shape, x....]
    unnamed x20 -> x6, local copies, waits for them, and re-layouts: 7.73 us -> 4.85 us
    pallas_call x1, Pallas kernels: 13.1 us -> 15.2 us  [backward(): pl.pallas_call(backward_kernel, grid=(KV,), out_shape=outs, in_specs=[sme...]
    pallas_call x1, Pallas kernels: 14.9 us -> 16.9 us  [collect(): pl.pallas_call(functools.partial(collect_kernel, devices), out_shape=jax....]
  transfers between devices with their start and end apart: 2 -> 2, of which waited for: 0 -> 0; matrix products, arithmetic and copies ran while one was open for 0% -> 0% of each run, Pallas kernels for 72% -> 73%
where the time goes in v3:
time: 82.6 us; the launch traced here: 81.8 us
  Pallas kernels  70.9 us (86%)
  local copies, waits for them, and re-layouts  4.85 us (6%)
  starting transfers between devices  4.01 us (5%)
  between operations  1.98 us (2%)
    pallas_call x1, Pallas kernels, share(): pl.pallas_call(functools.partial(share_kernel, devices), out_shape=(jax.S...  19.3 us
    pallas_call x1, Pallas kernels, collect(): pl.pallas_call(functools.partial(collect_kernel, devices), out_shape=jax....  16.9 us
    pallas_call x1, Pallas kernels, backward(): pl.pallas_call(backward_kernel, grid=(KV,), out_shape=outs, in_specs=[sme...  15.2 us
    pallas_call x1, Pallas kernels, forward(): pl.pallas_call(forward_kernel, out_shape=jax.ShapeDtypeStruct(x.shape, x....  11.5 us
    pallas_call x1, Pallas kernels, chances_call(): pl.pallas_call(chances_kernel, grid=(KV,), out_shape=(jax.ShapeDtypeStruc...  8.13 us
    unnamed x6, local copies, waits for them, and re-layouts  4.85 us
    ppermute x2, starting transfers between devices, shifted_2(): return lax.ppermute(value, axis, pairs)  4.01 us
  transfers between devices with their start and end apart: 2, of which 0 were waited for; matrix products, arithmetic and copies ran while one was open for 0% of the time, Pallas kernels for 73%

profile of v3, /device:TPU:0, one launch (start us, length us, event | category | flops | bytes accessed | tf_op | source)
XLA Modules:
  0.0 81.8 jit_solution(10688089188318042125)
XLA Ops:
  0.6 3.9 %collective-permute-start = (bf16[1,1,128,4096]{3,2,1,0:T(8,128)(2,1)}, bf16[1,1,128,4096]{3,2,1,0:T(8,128)(2,1)S(1)}, u32[]{:S(2)}, u32[]{:S(2)}) collective-permute-start(bf16[1,1,128,4096]{3,2,1,0:T(8,128)(2,1)} %param.12), channel_id=1, source_target_pairs={{0,24},{8,0},{16,8},{24,16},{1,25},{9,1},{17,9},{25,17},{2,26},{10... | collective-permute-start | bytes 3145736 | tf_op jit(solution)/shard_map/ppermute | solution.py:27
  4.6 16.9 %collect.1.pool = bf16[2,512,512]{2,1,0:T(8,128)(2,1)} custom-call(bf16[2,64,512]{2,1,0:T(8,128)(2,1)} %bitcast.15), custom_call_target="tpu_custom_call" | custom-call | flops 65536 | bytes 1048576 | tf_op jit(solution)/shard_map/collect/pallas_call | solution.py:358
  22.7 8.1 %chances.1 = (f32[4,384,1024]{2,1,0:T(8,128)}, bf16[128,4096]{1,0:T(8,128)(2,1)}, f32[128,128]{1,0:T(8,128)}, bf16[384,512]{1,0:T(8,128)(2,1)}, bf16[384,512]{1,0:T(8,128)(2,1)}) custom-call(s32[16]{0:T(128)} %bitcast.16, s32[1]{0:T(128)S(6)} %copy.18.length, bf16[128,4096]{1,0:T(8,128)(2,1)} %bitcast.19, f32[1,4096]{1,0:T(1,128)} %gain.5, ...), custom_call_target="tpu_custom_call" | custom-call | flops 402653184 | bytes 5242880 | tf_op jit(solution)/shard_map/chances/pallas_call | solution.py:436
  30.9 0.0 collective-permute-done
  30.9 0.0 copy-start.1
  30.9 0.1 collective-permute-start.1
  30.9 0.9 %copy-done.1 = bf16[1,1,128,4096]{3,2,1,0:T(8,128)(2,1)} copy-done((bf16[1,1,128,4096]{3,2,1,0:T(8,128)(2,1)}, bf16[1,1,128,4096]{3,2,1,0:T(8,128)(2,1)S(1)}, u32[]{:S(2)}) %copy-start.1) | copy-done | bytes 1048600
  31.8 15.2 %backward.1 = (bf16[128,4096]{1,0:T(8,128)(2,1)}, f32[2,512,512]{2,1,0:T(8,128)}, f32[2,128,512]{2,1,0:T(8,128)}, f32[1,4096]{1,0:T(1,128)}) custom-call(s32[16]{0:T(128)} %bitcast.17, s32[1]{0:T(128)S(6)} %copy.18.length, bf16[128,4096]{1,0:T(8,128)(2,1)} %bitcast.20, f32[1,4096]{1,0:T(1,128)} %gain.5, bf16[128,4096]{1,0:T(8,128)(2,1)} %bitcast.21, ...), custom_call_target="tpu_custom_call" | custom-call | flops 16106127360 | bytes 10485760 | tf_op jit(solution)/shard_map/backward/pallas_call | solution.py:473
  47.0 19.3 %share.1 = (f32[2,64,512]{2,1,0:T(8,128)}, f32[1,4096]{1,0:T(1,128)}) custom-call(f32[2,512,512]{2,1,0:T(8,128)} %get-tuple-element.28.part, f32[1,4096]{1,0:T(1,128)} %get-tuple-element.29.gain_part), custom_call_target="tpu_custom_call" | custom-call | flops 524288 | bytes 2097152 | tf_op jit(solution)/shard_map/share/pallas_call | solution.py:380
  66.3 0.0 collective-permute-done.1
  66.3 0.0 copy-start
  66.3 1.0 %copy-done = bf16[1,1,128,4096]{3,2,1,0:T(8,128)(2,1)} copy-done((bf16[1,1,128,4096]{3,2,1,0:T(8,128)(2,1)}, bf16[1,1,128,4096]{3,2,1,0:T(8,128)(2,1)S(1)}, u32[]{:S(2)}) %copy-start) | copy-done | bytes 1048600
  67.2 11.5 %forward.1 = bf16[128,4096]{1,0:T(8,128)(2,1)} custom-call(s32[16]{0:T(128)} %bitcast.18, s32[1]{0:T(128)S(6)} %copy.17.length, bf16[128,4096]{1,0:T(8,128)(2,1)} %bitcast.11, f32[1,4096]{1,0:T(1,128)} %gain.5, bf16[2,512,512]{2,1,0:T(8,128)(2,1)} %collect.1.pool, bf16[2,128,512]{2,1,0:T(8,128)(2,1)} %bitcast.13), custom_call_target="tpu_custom_call" | custom-call | flops 805306368 | bytes 2097152 | tf_op jit(solution)/shard_map/forward/pallas_call | solution.py:409
  78.8 1.7 %copy.19 = f32[1,2,64,512]{3,2,1,0:T(8,128)} copy(f32[1,2,64,512]{3,2,1,0:T(8,128)} %bitcast.14) | data formatting | bytes 524288
  80.4 1.3 %copy.20 = f32[1,4096]{1,0:T(1,128)} copy(f32[1,4096]{1,0:T(1,128)} %get-tuple-element.42) | data formatting | bytes 32768
Async XLA Ops:
  0.6 30.2 %collective-permute-start = (bf16[1,1,128,4096]{3,2,1,0:T(8,128)(2,1)}, bf16[1,1,128,4096]{3,2,1,0:T(8,128)(2,1)S(1)}, u32[]{:S(2)}, u32[]{:S(2)}) collective-permute-start(bf16[1,1,128,4096]{3,2,1,0:T(8,128)(2,1)} %param.12), channel_id=1, source_target_pairs={{0,24},{8,0},{16,8},{24,16},{1,25},{9,1},{17,9},{25,17},{2,26},{10... | collective-permute-start | bytes 3145736 | tf_op jit(solution)/shard_map/ppermute | solution.py:27
  30.9 1.0 %copy-start.1 = (bf16[1,1,128,4096]{3,2,1,0:T(8,128)(2,1)}, bf16[1,1,128,4096]{3,2,1,0:T(8,128)(2,1)S(1)}, u32[]{:S(2)}) copy-start(bf16[1,1,128,4096]{3,2,1,0:T(8,128)(2,1)S(1)} %collective-permute-done) | copy-start | bytes 3145732
  30.9 35.4 %collective-permute-start.1 = (bf16[1,1,128,4096]{3,2,1,0:T(8,128)(2,1)}, bf16[1,1,128,4096]{3,2,1,0:T(8,128)(2,1)S(1)}, u32[]{:S(2)}, u32[]{:S(2)}) collective-permute-start(bf16[1,1,128,4096]{3,2,1,0:T(8,128)(2,1)} %param.10), channel_id=1, source_target_pairs={{0,8},{8,16},{16,24},{24,0},{1,9},{9,17},{17,25},{25,1},{2,10},{10... | collective-permute-start | bytes 3145736 | tf_op jit(solution)/shard_map/ppermute | solution.py:27
  66.3 1.0 %copy-start = (bf16[1,1,128,4096]{3,2,1,0:T(8,128)(2,1)}, bf16[1,1,128,4096]{3,2,1,0:T(8,128)(2,1)S(1)}, u32[]{:S(2)}) copy-start(bf16[1,1,128,4096]{3,2,1,0:T(8,128)(2,1)S(1)} %collective-permute-done.1) | copy-start | bytes 3145732

commit v4 on v3

--- a/solution.py
+++ b/solution.py
@@ -18,7 +18,9 @@
 masked_score = -1e30
 scale = HD ** (-0.5)
 exp_scale = scale * math.log2(math.e)
-vmem_limit = 60 * 1024 * 1024
+vmem_limit = 52 * 1024 * 1024
+back_limit = 56 * 1024 * 1024
+wide_limit = 60 * 1024 * 1024
 
 
 def shifted_2(value, axis, steps):
@@ -85,24 +87,26 @@
 def forward_kernel(table, length, x, gain, pool, own, out, queries, keys, values):
     rows, width = x.shape
     group = width // KV
-    gather_rows(table, pool, own, keys, 0)
-    gather_rows(table, pool, own, values, 1)
-    norm_rows(x, gain, queries, None)
+    g = pl.program_id(0)
+
+    @pl.when(g == 0)
+    def _():
+        gather_rows(table, pool, own, keys, 0)
+        gather_rows(table, pool, own, values, 1)
+        norm_rows(x, gain, queries, None)
+
     mask = key_mask(rows, length[0])
     valid = (lax.broadcasted_iota(jnp.int32, (rows, HD), 0) < length[0]).astype(jnp.float32)
-
-    @pl.loop(0, KV)
-    def _(g):
-        columns = pl.ds(pl.multiple_of(g * HD, HD), HD)
-        k_group = keys[:, columns]
-        v_group = values[:, columns]
-        for h in range(0, group // HD, TOGETHER):
-            chances = chances_of(heads_of(queries, g, group, h, TOGETHER), k_group, mask)
-            attended = dot(v_group, chances.astype(jnp.bfloat16), 0, 0).T
-            for k in range(TOGETHER):
-                place = head_place(g, group, h + k)
-                piece = attended[k * rows : (k + 1) * rows]
-                out[:, place] = (x[:, place].astype(jnp.float32) + valid * piece).astype(out.dtype)
+    columns = pl.ds(pl.multiple_of(g * HD, HD), HD)
+    k_group = keys[:, columns]
+    v_group = values[:, columns]
+    for h in range(0, group // HD, TOGETHER):
+        chances = chances_of(heads_of(queries, g, group, h, TOGETHER), k_group, mask)
+        attended = dot(v_group, chances.astype(jnp.bfloat16), 0, 0).T
+        for k in range(TOGETHER):
+            floated = x[:, head_place(g, group, h + k)].astype(jnp.float32)
+            piece = attended[k * rows : (k + 1) * rows]
+            out[:, (h + k) * HD : (h + k + 1) * HD] = (floated + valid * piece).astype(out.dtype)
 
 
 def chances_kernel(table, length, x, gain, pool, own, chances, queries, inverses, keys, values):
@@ -205,6 +209,9 @@
     def after(d):
         return lax.rem(chip + d, chips)
 
+    def far(d):
+        return after(1 + lax.rem(chips // 2 + d - 2, chips - 1))
+
     def pair_copy(c):
         return pltpu.make_async_remote_copy(
             src_ref=part.at[:, slot(c, 1 - core), :], dst_ref=paired.at[c],
@@ -244,9 +251,11 @@
 
     gain_pair.start()
 
-    @pl.loop(1, chips + 1)
-    def _(d):
-        pair_copy(after(d)).start()
+    @pl.loop(1, chips)
+    def _(d):
+        pair_copy(far(d)).start()
+
+    pair_copy(chip).start()
 
     gain_pair.wait()
     gains[chip] = gain_part[...] + gain_paired[...]
@@ -257,7 +266,7 @@
 
     @pl.loop(1, chips)
     def _(d):
-        to = after(d)
+        to = far(d)
         pair_copy(to).wait()
         outgoing[to] = (part[:, slot(to, core), :] + paired[to]).astype(outgoing.dtype)
         chip_copy(to, chip).start()
@@ -301,6 +310,9 @@
     def after(d):
         return lax.rem(chip + d, chips)
 
+    def far(d):
+        return after(1 + lax.rem(chips // 2 + d - 2, chips - 1))
+
     def twin_copy(c, parity):
         return pltpu.make_async_remote_copy(
             src_ref=pool.at[:, slot(c, parity), :], dst_ref=pool.at[:, slot(c, parity), :],
@@ -328,7 +340,7 @@
 
     @pl.loop(1, chips)
     def _(d):
-        chip_copy(after(d), chip).start()
+        chip_copy(far(d), chip).start()
 
     pool[:, slot(chip, core), :] = part[...]
     twin_copy(chip, core).start()
@@ -404,13 +416,14 @@
 def forward(table, length, x, gain, pool, own):
     rows, width = x.shape
     count = table.shape[0] * BLOCK + rows
-    vmem = pl.BlockSpec(memory_space=pltpu.VMEM)
+    group = width // KV
     smem = pl.BlockSpec(memory_space=pltpu.SMEM)
     return pl.pallas_call(
         forward_kernel,
+        grid=(KV,),
         out_shape=jax.ShapeDtypeStruct(x.shape, x.dtype),
-        in_specs=[smem, smem] + [vmem] * 4,
-        out_specs=vmem,
+        in_specs=[smem, smem] + [whole_block(v.shape) for v in (x, gain, pool, own)],
+        out_specs=pl.BlockSpec((rows, group), lambda g: (0, g)),
         scratch_shapes=[
             pltpu.VMEM((rows, width), jnp.bfloat16),
             pltpu.VMEM((count, pool.shape[-1]), jnp.bfloat16),
@@ -451,7 +464,7 @@
             whole_block((count, pool.shape[-1])),
             whole_block((count, pool.shape[-1])),
         ),
-        compiler_params=pltpu.CompilerParams(vmem_limit_bytes=vmem_limit),
+        compiler_params=pltpu.CompilerParams(vmem_limit_bytes=wide_limit),
         cost_estimate=pl.CostEstimate(
             flops=2 * rows * width * count, bytes_accessed=10 * rows * width, transcendentals=rows * width // HD * count
         ),
@@ -487,7 +500,7 @@
             pltpu.VMEM((count, HD), jnp.float32),
             pltpu.VMEM((count, HD), jnp.float32),
         ],
-        compiler_params=pltpu.CompilerParams(vmem_limit_bytes=vmem_limit),
+        compiler_params=pltpu.CompilerParams(vmem_limit_bytes=back_limit),
         cost_estimate=pl.CostEstimate(
             flops=80 * rows * width * count, bytes_accessed=20 * rows * width, transcendentals=0
         ),

time: 82.6 us -> 79 us (0.956)
  Pallas kernels: 70.9 us -> 67.8 us
    pallas_call x1, Pallas kernels: 16.9 us -> 15 us  [collect(): pl.pallas_call(functools.partial(collect_kernel, devices), out_shape=jax....]
    unnamed x6 -> x16, local copies, waits for them, and re-layouts: 4.85 us -> 4.89 us
  transfers between devices with their start and end apart: 2 -> 2, of which waited for: 0 -> 0; matrix products, arithmetic and copies ran while one was open for 0% -> 0% of each run, Pallas kernels for 73% -> 72%
where the time goes in v4:
time: 79 us; the launch traced here: 78.7 us
  Pallas kernels  67.8 us (86%)
  local copies, waits for them, and re-layouts  4.89 us (6%)
  starting transfers between devices  4.01 us (5%)
  between operations  2.01 us (3%)
    pallas_call x1, Pallas kernels, share(): pl.pallas_call(functools.partial(share_kernel, devices), out_shape=(jax.S...  18.5 us
    pallas_call x1, Pallas kernels, backward(): pl.pallas_call(backward_kernel, grid=(KV,), out_shape=outs, in_specs=[sme...  15.2 us
    pallas_call x1, Pallas kernels, collect(): pl.pallas_call(functools.partial(collect_kernel, devices), out_shape=jax....  15 us
    pallas_call x1, Pallas kernels, forward(): pl.pallas_call(forward_kernel, grid=(KV,), out_shape=jax.ShapeDtypeStruct...  10.9 us
    pallas_call x1, Pallas kernels, chances_call(): pl.pallas_call(chances_kernel, grid=(KV,), out_shape=(jax.ShapeDtypeStruc...  8.14 us
    unnamed x16, local copies, waits for them, and re-layouts  4.89 us
    ppermute x2, starting transfers between devices, shifted_2(): return lax.ppermute(value, axis, pairs)  4.01 us
  transfers between devices with their start and end apart: 2, of which 0 were waited for; matrix products, arithmetic and copies ran while one was open for 0% of the time, Pallas kernels for 72%

profile of v4, /device:TPU:0, one launch (start us, length us, event | category | flops | bytes accessed | tf_op | source)
XLA Modules:
  0.0 78.7 jit_solution(4385003668284064351)
XLA Ops:
  0.6 3.9 %collective-permute-start = (bf16[1,1,128,4096]{3,2,1,0:T(8,128)(2,1)}, bf16[1,1,128,4096]{3,2,1,0:T(8,128)(2,1)S(1)}, u32[]{:S(2)}, u32[]{:S(2)}) collective-permute-start(bf16[1,1,128,4096]{3,2,1,0:T(8,128)(2,1)} %param.12), channel_id=1, source_target_pairs={{0,24},{8,0},{16,8},{24,16},{1,25},{9,1},{17,9},{25,17},{2,26},{10... | collective-permute-start | bytes 3145736 | tf_op jit(solution)/shard_map/ppermute | solution.py:29
  4.6 0.0 copy-start.2
  4.6 0.9 %copy-done.2 = bf16[1,2,64,512]{3,2,1,0:T(8,128)(2,1)S(1)} copy-done((bf16[1,2,64,512]{3,2,1,0:T(8,128)(2,1)S(1)}, bf16[1,2,64,512]{3,2,1,0:T(8,128)(2,1)}, u32[]{:S(2)}) %copy-start.2) | copy-done | bytes 131096
  5.5 15.0 %collect.1.pool = bf16[2,512,512]{2,1,0:T(8,128)(2,1)S(1)} custom-call(bf16[2,64,512]{2,1,0:T(8,128)(2,1)S(1)} %bitcast.14), custom_call_target="tpu_custom_call" | custom-call | flops 65536 | bytes 1048576 | tf_op jit(solution)/shard_map/collect/pallas_call | solution.py:370
  20.5 0.0 copy-start
  20.5 1.1 %copy-done = bf16[2,512,512]{2,1,0:T(8,128)(2,1)} copy-done((bf16[2,512,512]{2,1,0:T(8,128)(2,1)}, bf16[2,512,512]{2,1,0:T(8,128)(2,1)S(1)}, u32[]{:S(2)}) %copy-start) | copy-done | bytes 1048600
  22.9 8.1 %chances.1 = (f32[4,384,1024]{2,1,0:T(8,128)}, bf16[128,4096]{1,0:T(8,128)(2,1)}, f32[128,128]{1,0:T(8,128)}, bf16[384,512]{1,0:T(8,128)(2,1)}, bf16[384,512]{1,0:T(8,128)(2,1)}) custom-call(s32[16]{0:T(128)} %bitcast.15, s32[1]{0:T(128)S(6)} %copy.18.length, bf16[128,4096]{1,0:T(8,128)(2,1)} %bitcast.19, f32[1,4096]{1,0:T(1,128)} %gain.5, ...), custom_call_target="tpu_custom_call" | custom-call | flops 402653184 | bytes 5242880 | tf_op jit(solution)/shard_map/chances/pallas_call | solution.py:449
  31.0 0.0 collective-permute-done
  31.0 0.0 copy-start.6
  31.0 0.1 collective-permute-start.1
  31.1 0.9 %copy-done.6 = bf16[1,1,128,4096]{3,2,1,0:T(8,128)(2,1)} copy-done((bf16[1,1,128,4096]{3,2,1,0:T(8,128)(2,1)}, bf16[1,1,128,4096]{3,2,1,0:T(8,128)(2,1)S(1)}, u32[]{:S(2)}) %copy-start.6) | copy-done | bytes 1048600
  32.0 0.0 copy-start.1
  32.0 0.0 copy-start.3
  32.0 0.0 copy-start.5
  32.0 15.2 %backward.1 = (bf16[128,4096]{1,0:T(8,128)(2,1)}, f32[2,512,512]{2,1,0:T(8,128)}, f32[2,128,512]{2,1,0:T(8,128)}, f32[1,4096]{1,0:T(1,128)}) custom-call(s32[16]{0:T(128)} %bitcast.16, s32[1]{0:T(128)S(6)} %copy.18.length, bf16[128,4096]{1,0:T(8,128)(2,1)} %bitcast.20, f32[1,4096]{1,0:T(1,128)} %gain.5, bf16[128,4096]{1,0:T(8,128)(2,1)} %bitcast.21, ...), custom_call_target="tpu_custom_call" | custom-call | flops 16106127360 | bytes 10485760 | tf_op jit(solution)/shard_map/backward/pallas_call | solution.py:486
  47.2 0.0 copy-start.4
  47.2 0.7 copy-done.4
  47.9 18.5 %share.1 = (f32[2,64,512]{2,1,0:T(8,128)S(1)}, f32[1,4096]{1,0:T(1,128)S(1)}) custom-call(f32[2,512,512]{2,1,0:T(8,128)} %get-tuple-element.28.part, f32[1,4096]{1,0:T(1,128)S(1)} %copy-done.4), custom_call_target="tpu_custom_call" | custom-call | flops 524288 | bytes 2097152 | tf_op jit(solution)/shard_map/share/pallas_call | solution.py:392
  66.4 0.0 collective-permute-done.1
  66.4 0.0 copy-done.1
  66.4 0.0 copy-done.3
  66.5 0.0 copy-done.5
  66.5 10.9 %forward.1 = bf16[128,4096]{1,0:T(8,128)(2,1)} custom-call(s32[16]{0:T(128)S(1)} %bitcast.17, s32[1]{0:T(128)S(6)} %copy.17.length, bf16[128,4096]{1,0:T(8,128)(2,1)S(1)} %bitcast.11, f32[1,4096]{1,0:T(1,128)S(1)} %copy-done.3, bf16[2,512,512]{2,1,0:T(8,128)(2,1)} %copy-done, bf16[2,128,512]{2,1,0:T(8,128)(2,1)S(1)} %bitcast.12), custom_call_target="tpu_custom_call" | custom-call | flops 805306368 | bytes 2097152 | tf_op jit(solution)/shard_map/forward/pallas_call | solution.py:421
  77.4 0.7 copy.19
  78.1 0.6 copy.20
Async XLA Ops:
  0.6 30.4 %collective-permute-start = (bf16[1,1,128,4096]{3,2,1,0:T(8,128)(2,1)}, bf16[1,1,128,4096]{3,2,1,0:T(8,128)(2,1)S(1)}, u32[]{:S(2)}, u32[]{:S(2)}) collective-permute-start(bf16[1,1,128,4096]{3,2,1,0:T(8,128)(2,1)} %param.12), channel_id=1, source_target_pairs={{0,24},{8,0},{16,8},{24,16},{1,25},{9,1},{17,9},{25,17},{2,26},{10... | collective-permute-start | bytes 3145736 | tf_op jit(solution)/shard_map/ppermute | solution.py:29
  4.6 0.9 %copy-start.2 = (bf16[1,2,64,512]{3,2,1,0:T(8,128)(2,1)S(1)}, bf16[1,2,64,512]{3,2,1,0:T(8,128)(2,1)}, u32[]{:S(2)}) copy-start(bf16[1,2,64,512]{3,2,1,0:T(8,128)(2,1)} %param.13) | copy-start | bytes 393220
  20.5 1.1 %copy-start = (bf16[2,512,512]{2,1,0:T(8,128)(2,1)}, bf16[2,512,512]{2,1,0:T(8,128)(2,1)S(1)}, u32[]{:S(2)}) copy-start(bf16[2,512,512]{2,1,0:T(8,128)(2,1)S(1)} %collect.1.pool) | copy-start | bytes 3145732
  31.0 1.0 %copy-start.6 = (bf16[1,1,128,4096]{3,2,1,0:T(8,128)(2,1)}, bf16[1,1,128,4096]{3,2,1,0:T(8,128)(2,1)S(1)}, u32[]{:S(2)}) copy-start(bf16[1,1,128,4096]{3,2,1,0:T(8,128)(2,1)S(1)} %collective-permute-done) | copy-start | bytes 3145732
  31.0 35.4 %collective-permute-start.1 = (bf16[1,1,128,4096]{3,2,1,0:T(8,128)(2,1)}, bf16[1,1,128,4096]{3,2,1,0:T(8,128)(2,1)S(1)}, u32[]{:S(2)}, u32[]{:S(2)}) collective-permute-start(bf16[1,1,128,4096]{3,2,1,0:T(8,128)(2,1)} %param.10), channel_id=1, source_target_pairs={{0,8},{8,16},{16,24},{24,0},{1,9},{9,17},{17,25},{25,1},{2,10},{10... | collective-permute-start | bytes 3145736 | tf_op jit(solution)/shard_map/ppermute | solution.py:29
  32.0 34.4 %copy-start.1 = (bf16[1,1,2,128,512]{4,3,2,1,0:T(8,128)(2,1)S(1)}, bf16[1,1,2,128,512]{4,3,2,1,0:T(8,128)(2,1)}, u32[]{:S(2)}) copy-start(bf16[1,1,2,128,512]{4,3,2,1,0:T(8,128)(2,1)} %param.14) | copy-start | bytes 786436
  32.0 34.4 %copy-start.3 = (f32[1,4096]{1,0:T(1,128)S(1)}, f32[1,4096]{1,0:T(1,128)}, u32[]{:S(2)}) copy-start(f32[1,4096]{1,0:T(1,128)} %gain.5) | copy-start | bytes 49156
  32.0 34.4 %copy-start.5 = (s32[1,16]{1,0:T(1,128)S(1)}, s32[1,16]{1,0:T(1,128)}, u32[]{:S(2)}) copy-start(s32[1,16]{1,0:T(1,128)} %param.17) | copy-start | bytes 196
  47.2 0.7 copy-start.4
